TPU v7x, 512 devices: a whole 4x8x8 slice. The times are simulated.
512 devices in a mesh: dp: 128 (over y, z_hi, x), mp: 4 (over z_lo, core).
Axes of the slice: x: 4, y: 8, z: 8 (z_hi: 4, z_lo: 2; z = z_hi * 2 + z_lo), core: 2. Of those that a mesh axis runs over, the one named last changes fastest.
Arguments:
- frames: bfloat16 [2048, 32, 1408], P('dp', None, 'mp'), may hold values from -6 to 6
- frame_counts: int32 [2048], P('dp'), may hold values from 1 to 32, 32768 in all
- norm_gain: float32 [1408], replicated, may hold values from 0.5 to 1.5
- norm_bias: float32 [1408], replicated, may hold values from -3 to 3
- up_weight: bfloat16 [1408, 3072], P('dp', 'mp'), may hold values from -0.15625 to 0.15625
- up_bias: float32 [3072], P('mp'), may hold values from -3 to 3
- down_weight: bfloat16 [1408, 3072], P('dp', 'mp'), may hold values from -0.109375 to 0.109375
- down_bias: float32 [1408], replicated, may hold values from -3 to 3
- final_gain: float32 [1408], P('mp'), may hold values from 0.5 to 1.5
- final_bias: float32 [1408], P('mp'), may hold values from -3 to 3
- projection: bfloat16 [1408, 1024], P('mp'), may hold values from -0.15625 to 0.15625
- captions: bfloat16 [2048, 1024], P(('dp', 'mp')), may hold values from -6 to 6
- positives: int32 [2048], P('dp'), may hold values from 0 to 2047, each once
- logit_scale: float32 [], replicated, may hold values from 8 to 16
- logit_bias: float32 [], replicated, may hold values from -5 to -2
Outputs:
- video_embed: float32 [2048, 1024], P('dp')
- video_grad: float32 [2048, 1024], P('dp')
- text_grad: float32 [2048, 1024], P(('dp', 'mp'))
Inputs may be any that keep to these rules, and one draw needn't show every extreme that they name: `frame_counts`: the counts sum to 32768, and some clip has 32 frames. `positives`: every caption is the match of exactly one clip.
All inputs are finite; a program needn't handle non-finite values. No bound on the sum of `frame_counts` on one device may be relied on, other than what follows from the above.
Results may differ from a plain program's by a relative error of at most 0.015.
Values may be sent and summed in bfloat16 or wider, within the bound.
A program may use at most 64 MiB of HBM per device.

v0:
```python
import jax
import jax.numpy as jnp
from jax import lax
from jax.sharding import PartitionSpec as P

D = 1408


epsilon = 1e-06


def on_device(
    frames,
    frame_counts,
    norm_gain,
    norm_bias,
    up_weight,
    up_bias,
    down_weight,
    down_bias,
    final_gain,
    final_bias,
    projection,
    captions,
    positives,
    logit_scale,
    logit_bias,
):
    clip_count, slot_count, local_width = frames.shape
    row_count = clip_count * slot_count
    gathered = lax.all_gather(frames, "mp", axis=2, tiled=True)
    frame_rows = gathered.reshape(row_count, D).astype(jnp.float32)
    row_mean = jnp.mean(frame_rows, axis=-1, keepdims=True)
    square_mean = jnp.mean(frame_rows * frame_rows, axis=-1, keepdims=True)
    normed = (
        (frame_rows - row_mean) * lax.rsqrt(square_mean - row_mean * row_mean + epsilon) * norm_gain
        + norm_bias
    ).astype(jnp.bfloat16)
    up_sum = jnp.dot(
        normed,
        lax.all_gather(up_weight, "dp", axis=0, tiled=True),
        preferred_element_type=jnp.float32,
    )
    hidden = jax.nn.gelu(up_sum + up_bias, approximate=False).astype(jnp.bfloat16)
    partial_value = lax.dot_general(
        hidden,
        lax.all_gather(down_weight, "dp", axis=0, tiled=True),
        (((1,), (1,)), ((), ())),
        preferred_element_type=jnp.float32,
    )
    feature_offset = lax.axis_index("mp") * local_width
    summed = lax.psum(partial_value.astype(jnp.bfloat16), "mp").astype(jnp.float32)
    resid = frame_rows + summed + down_bias
    resid_mean = jnp.mean(resid, axis=-1, keepdims=True)
    resid_square = jnp.mean(resid * resid, axis=-1, keepdims=True)
    whole_scaled = (resid - resid_mean) * lax.rsqrt(
        resid_square - resid_mean * resid_mean + epsilon
    )
    scaled = lax.dynamic_slice_in_dim(whole_scaled, feature_offset, local_width, 1)
    final_rows = (scaled * final_gain + final_bias).reshape(clip_count, slot_count, local_width)
    frame_mask = (jnp.arange(slot_count, dtype=jnp.int32)[None, :] < frame_counts[:, None]).astype(
        jnp.float32
    )
    pooled = jnp.sum(final_rows * frame_mask[:, :, None], axis=1) / frame_counts[:, None].astype(
        jnp.float32
    )
    pooled = pooled.astype(jnp.bfloat16)
    raw = lax.psum(
        jnp.dot(pooled, projection, preferred_element_type=jnp.float32).astype(jnp.bfloat16), "mp"
    ).astype(jnp.float32)
    video_embed = raw * lax.rsqrt(jnp.sum(raw * raw, axis=-1, keepdims=True) + epsilon)
    video_unit = video_embed.astype(jnp.bfloat16)
    caption_values = captions.astype(jnp.float32)
    text_unit = (
        caption_values
        * lax.rsqrt(jnp.sum(caption_values * caption_values, axis=-1, keepdims=True) + epsilon)
    ).astype(jnp.bfloat16)
    text_column = lax.all_gather(text_unit, "dp", axis=0, tiled=True)
    caption_rows = captions.shape[0]
    dp_count = lax.axis_size("dp")
    mp_count = lax.axis_size("mp")
    column_pos = jnp.arange(dp_count * caption_rows, dtype=jnp.int32)
    owner_dp = column_pos // caption_rows
    within_row = column_pos % caption_rows
    column_ids = (owner_dp * mp_count + lax.axis_index("mp")) * caption_rows + within_row
    labels = jnp.where(
        column_ids[None, :] == positives[:, None], jnp.float32(1.0), jnp.float32(-1.0)
    )
    logits = (
        logit_scale
        * lax.dot_general(
            video_unit, text_column, (((1,), (1,)), ((), ())), preferred_element_type=jnp.float32
        )
        + logit_bias
    )
    pair_weights = (-labels * jax.nn.sigmoid(-labels * logits)).astype(jnp.bfloat16)
    video_part = logit_scale * jnp.dot(
        pair_weights, text_column, preferred_element_type=jnp.float32
    )
    text_part = logit_scale * lax.dot_general(
        pair_weights, video_unit, (((0,), (0,)), ((), ())), preferred_element_type=jnp.float32
    )
    text_grad = lax.psum_scatter(text_part, "dp", scatter_dimension=0, tiled=True)
    video_grad = lax.psum(video_part.astype(jnp.bfloat16), "mp").astype(jnp.float32)
    return (video_embed, video_grad, text_grad)


def solution(mesh):
    return jax.shard_map(
        on_device,
        mesh=mesh,
        in_specs=(
            P("dp", None, "mp"),
            P("dp"),
            P(),
            P(),
            P("dp", "mp"),
            P("mp"),
            P("dp", "mp"),
            P(),
            P("mp"),
            P("mp"),
            P("mp", None),
            P(("dp", "mp"), None),
            P("dp"),
            P(),
            P(),
        ),
        out_specs=(P("dp", None), P("dp", None), P(("dp", "mp"), None)),
        check_vma=False,
    )
```

profile of v0, /device:TPU:6, one launch (start us, length us, event | category | flops | bytes accessed | tf_op | source)
XLA Modules:
  0.0 1987.5 jit_solution(719603122979283261)
XLA Ops:
  7.2 2.8 copy.18
  10.1 0.7 all-gather.10.cloned.1.call-update
  10.8 0.7 all-gather.12.cloned.1.call-update
  11.6 0.1 fusion.59
  11.7 0.7 fusion.64
  12.5 66.6 %all-gather.8.cloned.1.call-done = bf16[16,32,1408]{1,0,2:T(8,128)(2,1)} async-done(((bf16[16,32,352]{1,0,2:T(8,128)(2,1)}), bf16[16,32,1408]{1,0,2:T(8,128)(2,1)}) %all-gather.8.cloned.1.call-update) | async-done | bytes 1441808 | tf_op jit(solution)/shard_map/all_gather | solution.py:31
  79.1 4.7 convert_reduce_fusion
  83.8 0.1 div.36
  84.0 7.8 copy.19
  91.8 3.5 fusion.3
  95.2 116.9 %all-gather.10.cloned.1.call-done = bf16[128,11,768]{2,1,0:T(8,128)(2,1)} async-done(((bf16[1,11,768]{2,1,0:T(8,128)(2,1)}), bf16[128,11,768]{2,1,0:T(8,128)(2,1)}) %all-gather.10.cloned.1.call-update) | async-done | bytes 2162704 | tf_op jit(solution)/shard_map/all_gather | solution.py:41
  212.1 3.0 reshape.132
  215.1 124.4 %all-gather.12.cloned.1.call-done = bf16[128,11,768]{2,1,0:T(8,128)(2,1)} async-done(((bf16[1,11,768]{2,1,0:T(8,128)(2,1)}), bf16[128,11,768]{2,1,0:T(8,128)(2,1)}) %all-gather.12.cloned.1.call-update) | async-done | bytes 2162704 | tf_op jit(solution)/shard_map/all_gather | solution.py:47
  339.6 4.4 reshape.134
  344.0 9.4 convolution_convert_fusion
  354.9 100.3 %all-gather.14.cloned.1.call-done = bf16[128,4,1024]{2,1,0:T(4,128)(2,1)} async-done(((bf16[1,4,1024]{2,1,0:T(4,128)(2,1)}), bf16[128,4,1024]{2,1,0:T(4,128)(2,1)}) %all-gather.14.cloned.1.call-update) | async-done | bytes 1048592 | tf_op jit(solution)/shard_map/all_gather | solution.py:78
  455.2 1.3 reshape.136
  456.6 54.1 %all-reduce.4.cloned.1.call-done = bf16[512,1408]{1,0:T(8,128)(2,1)} async-done(((bf16[512,1408]{1,0:T(8,128)(2,1)}), bf16[512,1408]{1,0:T(8,128)(2,1)}) %all-reduce.4.cloned.1.call-update) | async-done | bytes 1441808 | tf_op jit(solution)/shard_map/psum | solution.py:52
  510.7 2.9 fusion.107
  513.6 0.5 multiply_reduce_fusion.2
  514.2 0.3 convolution_convert_fusion.1
  514.4 10.3 psum.22
  524.7 0.1 fusion.58
  524.8 0.1 convert_multiply_fusion
  524.9 0.4 fusion.23
  525.3 1.8 convolution_multiply_fusion
  527.1 1.3 dynamic-slice
  529.0 0.3 fusion.15
  529.3 10.3 psum.23
  539.6 0.6 convert_element_type.77
  540.2 1439.0 %all-reduce.6.cloned.1.call-done = f32[512,1024]{1,0:T(8,128)} async-done(((f32[512,1024]{1,0:T(8,128)}), f32[512,1024]{1,0:T(8,128)}) %all-reduce.6.cloned.1.call-update) | async-done | bytes 2097168
  1979.2 1.4 constant_dynamic-slice_fusion
  (41 shorter events, 0.6 us)
Async XLA Ops:
  7.2 507.0 %copy-start = (bf16[352,1024]{1,0:T(8,128)(2,1)S(1)}, bf16[352,1024]{1,0:T(8,128)(2,1)}, u32[]{:S(2)}) copy-start(bf16[352,1024]{1,0:T(8,128)(2,1)} %param.25) | copy-start | bytes 2162692
  7.2 4.4 copy-start.2
  7.2 71.9 %all-gather.8.cloned.1.call-start = ((), (), s32[]{:S(2)}) async-start(), calls=%async_computation | async-start | bytes 7208960 | tf_op jit(solution)/shard_map/all_gather | solution.py:31
  10.0 202.1 %all-gather.10.cloned.1.call-start = ((), (), s32[]{:S(2)}) async-start(), calls=%async_computation.2 | async-start | bytes 3170304 | tf_op jit(solution)/shard_map/all_gather | solution.py:41
  10.8 328.8 %all-gather.12.cloned.1.call-start = ((), (), s32[]{:S(2)}) async-start(), calls=%async_computation.3 | async-start | bytes 3170304 | tf_op jit(solution)/shard_map/all_gather | solution.py:47
  11.5 443.7 %all-gather.14.cloned.1.call-start = ((), (), s32[]{:S(2)}) async-start(), calls=%async_computation.4 | async-start | bytes 1056768 | tf_op jit(solution)/shard_map/all_gather | solution.py:78
  12.4 498.2 %all-reduce.4.cloned.1.call-start = ((), (), s32[]{:S(2)}) async-start(), calls=%async_computation.1 | async-start | bytes 2883584 | tf_op jit(solution)/shard_map/psum | solution.py:52
  84.0 7.8 copy-start.3
  84.0 7.8 copy-start.4
  215.1 128.9 %copy-start.10 = (f32[768]{0:T(1024)S(1)}, f32[768]{0:T(1024)}, u32[]{:S(2)}) copy-start(f32[768]{0:T(1024)} %param.20) | copy-start | bytes 9220
  344.0 9.5 copy-start.9
  353.4 157.3 %copy-start.5 = (f32[1408]{0:T(1024)S(1)}, f32[1408]{0:T(1024)}, u32[]{:S(2)}) copy-start(f32[1408]{0:T(1024)} %param.22) | copy-start | bytes 16900
  353.4 1625.8 %all-reduce.6.cloned.1.call-start = ((), (), s32[]{:S(2)}) async-start(), calls=%async_computation.5 | async-start | bytes 4194304
  456.5 57.0 %copy-start.6 = (f32[352]{0:T(512)S(1)}, f32[352]{0:T(512)}, u32[]{:S(2)}) copy-start(f32[352]{0:T(512)} %param.24) | copy-start | bytes 4228
  456.6 57.0 %copy-start.7 = (f32[352]{0:T(512)S(1)}, f32[352]{0:T(512)}, u32[]{:S(2)}) copy-start(f32[352]{0:T(512)} %param.23) | copy-start | bytes 4228
  513.6 11.3 copy-start.8
  524.9 2.2 copy-start.1
Sparse Core Ops, SparseCore 0:
  10.1 68.8 all-gather.7
  83.6 128.4 all-gather.9
  216.7 122.8 all-gather.11
  344.4 110.7 all-gather.13
  458.0 52.5 all-reduce.3
  527.2 1451.9 all-reduce.5
where the time goes:
time: 1990 us
  waiting for transfers between devices  1900 us (95%)
  local copies, waits for them, and re-layouts  22.1 us (1%)
  blocking collectives  20.5 us (1%)
    unnamed x7, waiting for transfers between devices  1440 us
    all_gather x1, waiting for transfers between devices, on_device(): lax.all_gather(down_weight, 'dp', axis=0, tiled=True)  124 us
    all_gather x1, waiting for transfers between devices, on_device(): lax.all_gather(up_weight, 'dp', axis=0, tiled=True)  117 us
    all_gather x1, waiting for transfers between devices, on_device(): text_column = lax.all_gather(text_unit, 'dp', axis=0, tiled=True)  100 us
    all_gather x1, waiting for transfers between devices, on_device(): gathered = lax.all_gather(frames, 'mp', axis=2, tiled=True)  66.6 us
    psum x1, waiting for transfers between devices, on_device(): lax.psum(partial_value.astype(jnp.bfloat16), 'mp').astype(jnp.float32)  54.1 us
  transfers between devices with their start and end apart: 6, of which 6 were waited for; matrix products, arithmetic and copies ran while one was open for 2% of the time, Pallas kernels for 0%

commit v1 on v0

--- a/solution.py
+++ b/solution.py
@@ -1,12 +1,239 @@
+import functools
+
 import jax
 import jax.numpy as jnp
 from jax import lax
+from jax.experimental import pallas as pl
+from jax.experimental.pallas import tpu as pltpu
 from jax.sharding import PartitionSpec as P
 
 D = 1408
-
-
+E = 1024
+NY, NZ, NX, NM = 8, 4, 4, 4
+MESH = pl.DeviceIdType.MESH
 epsilon = 1e-06
+F32 = jnp.float32
+BF16 = jnp.bfloat16
+
+
+def position():
+    dp = lax.axis_index("dp")
+    mp = lax.axis_index("mp")
+    return dp // (NZ * NX), (dp // NX) % NZ, dp % NX, mp
+
+
+def device(y, z, x, m):
+    return ((y * NZ + z) * NX + x, m)
+
+
+def peer_at(axis, step):
+    y, z, x, m = position()
+    if axis == "y":
+        place = (y + step) % NY
+        return device(place, z, x, m), place
+    if axis == "z":
+        place = (z + step) % NZ
+        return device(y, place, x, m), place
+    if axis == "x":
+        place = (x + step) % NX
+        return device(y, z, place, m), place
+    place = (m + step) % NM
+    return device(y, z, x, place), place
+
+
+SIZES = {"y": NY, "z": NZ, "x": NX, "m": NM}
+
+
+def greet():
+    barrier = pltpu.get_barrier_semaphore()
+    total = 0
+    for axis, size in SIZES.items():
+        for step in range(1, size):
+            target, _ = peer_at(axis, step)
+            pl.semaphore_signal(barrier, inc=1, device_id=target, device_id_type=MESH)
+            total += 1
+    pl.semaphore_wait(barrier, total)
+
+
+class Exchange:
+    def __init__(self, axis, source, slots, send_sem, recv_sem):
+        self.axis, self.source, self.slots = axis, source, slots
+        self.send_sem, self.recv_sem = send_sem, recv_sem
+        y, z, x, m = position()
+        self.own = {"y": y, "z": z, "x": x, "m": m}[axis]
+
+    def copy(self, step):
+        target, place = peer_at(self.axis, step)
+        return pltpu.make_async_remote_copy(
+            src_ref=self.source(place),
+            dst_ref=self.slots.at[self.own],
+            send_sem=self.send_sem.at[step],
+            recv_sem=self.recv_sem.at[self.own],
+            device_id=target,
+            device_id_type=MESH,
+        )
+
+    def start(self):
+        for step in range(1, SIZES[self.axis]):
+            self.copy(step).start()
+
+    def wait(self):
+        for step in range(1, SIZES[self.axis]):
+            target, place = peer_at(self.axis, step)
+            pltpu.make_async_remote_copy(
+                src_ref=self.source(place),
+                dst_ref=self.slots.at[place],
+                send_sem=self.send_sem.at[step],
+                recv_sem=self.recv_sem.at[place],
+                device_id=target,
+                device_id_type=MESH,
+            ).wait_recv()
+        for step in range(1, SIZES[self.axis]):
+            self.copy(step).wait_send()
+
+
+def loss_kernel(
+    raw_ref,
+    captions_ref,
+    positives_ref,
+    scalars_ref,
+    embed_ref,
+    video_ref,
+    text_ref,
+    text_z,
+    text_rows,
+    text_y,
+    video_x,
+    where_x,
+    text_out,
+    text_in,
+    video_out,
+    video_in,
+    text_sum,
+    text_part,
+    text_last,
+    mp_in,
+    send_sems,
+    recv_sems,
+):
+    y, z, x, m = position()
+    scale = scalars_ref[0]
+    bias = scalars_ref[1]
+    greet()
+    caption_values = captions_ref[...].astype(F32)
+    text_unit = caption_values * lax.rsqrt(
+        jnp.sum(caption_values * caption_values, axis=-1, keepdims=True) + epsilon
+    )
+    text_z[z] = text_unit
+    gather_text_z = Exchange("z", lambda place: text_z.at[z], text_z, send_sems.at[0], recv_sems.at[0])
+    gather_text_z.start()
+    where_x[x] = positives_ref[...]
+    gather_where = Exchange("x", lambda place: where_x.at[x], where_x, send_sems.at[1], recv_sems.at[1])
+    gather_where.start()
+    raw = raw_ref[...]
+    embed = raw * lax.rsqrt(jnp.sum(raw * raw, axis=-1, keepdims=True) + epsilon)
+    embed_ref[...] = embed
+    video_x[x] = embed.astype(BF16)
+    gather_video = Exchange("x", lambda place: video_x.at[x], video_x, send_sems.at[2], recv_sems.at[2])
+    gather_video.start()
+    gather_text_z.wait()
+    for slot in range(NZ):
+        text_rows[4 * slot : 4 * slot + 4, :] = text_z[slot]
+    text_y[y] = text_rows[...].astype(BF16)
+    gather_text_y = Exchange("y", lambda place: text_y.at[y], text_y, send_sems.at[3], recv_sems.at[3])
+    gather_text_y.start()
+    gather_where.wait()
+    gather_video.wait()
+    gather_text_y.wait()
+
+    text = text_y[...].reshape(NY * 16, E)
+    video = video_x[...].reshape(NX * 16, E)
+    logits = scale * lax.dot_general(
+        video, text, (((1,), (1,)), ((), ())), preferred_element_type=F32
+    ) + bias
+    column = lax.broadcasted_iota(jnp.int32, (NX * 16, NY * 16), 1)
+    owner = lax.shift_right_logical(column, 2)
+    ids = (((owner * 4) + x) * 4 + m) * 4 + lax.bitwise_and(column, 3)
+    labels = jnp.where(ids == where_x[...].reshape(NX * 16, 128), F32(1.0), F32(-1.0))
+    pair_weights = -labels * lax.logistic(-labels * logits)
+    turned = jnp.transpose(pair_weights).astype(BF16)
+    text_terms = scale * jnp.dot(turned, video, preferred_element_type=F32)
+    text_out[...] = text_terms.astype(BF16).reshape(NY, 16, E)
+    text_in[y] = text_out[y]
+    reduce_text_y = Exchange("y", lambda place: text_out.at[place], text_in, send_sems.at[4], recv_sems.at[4])
+    reduce_text_y.start()
+    video_terms = scale * jnp.dot(pair_weights.astype(BF16), text, preferred_element_type=F32)
+    video_out[...] = video_terms.astype(BF16).reshape(NX, 16, E)
+    video_in[x] = video_out[x]
+    reduce_video_x = Exchange("x", lambda place: video_out.at[place], video_in, send_sems.at[5], recv_sems.at[5])
+    reduce_video_x.start()
+
+    reduce_video_x.wait()
+    video_total = video_in[0].astype(F32)
+    for slot in range(1, NX):
+        video_total += video_in[slot].astype(F32)
+    mp_in[m] = video_total.astype(BF16)
+    share_video = Exchange("m", lambda place: mp_in.at[m], mp_in, send_sems.at[6], recv_sems.at[6])
+    share_video.start()
+    reduce_text_y.wait()
+    text_total = text_in[0].astype(F32)
+    for slot in range(1, NY):
+        text_total += text_in[slot].astype(F32)
+    text_sum[...] = text_total
+    for slot in range(NZ):
+        text_part[slot] = text_sum[4 * slot : 4 * slot + 4, :]
+    text_last[z] = text_part[z]
+    reduce_text_z = Exchange("z", lambda place: text_part.at[place], text_last, send_sems.at[7], recv_sems.at[7])
+    reduce_text_z.start()
+    share_video.wait()
+    video_grad = mp_in[0].astype(F32)
+    for slot in range(1, NM):
+        video_grad += mp_in[slot].astype(F32)
+    video_ref[...] = video_grad
+    reduce_text_z.wait()
+    text_grad = text_last[0]
+    for slot in range(1, NZ):
+        text_grad += text_last[slot]
+    text_ref[...] = text_grad
+
+
+def loss_part(raw, captions, positives, logit_scale, logit_bias):
+    vmem = pl.BlockSpec(memory_space=pltpu.VMEM)
+    return pl.pallas_call(
+        loss_kernel,
+        out_shape=(
+            jax.ShapeDtypeStruct((16, E), F32),
+            jax.ShapeDtypeStruct((16, E), F32),
+            jax.ShapeDtypeStruct((4, E), F32),
+        ),
+        in_specs=[vmem, vmem, vmem, pl.BlockSpec(memory_space=pltpu.SMEM)],
+        out_specs=(vmem, vmem, vmem),
+        scratch_shapes=[
+            pltpu.VMEM((NZ, 4, E), F32),
+            pltpu.VMEM((16, E), F32),
+            pltpu.VMEM((NY, 16, E), BF16),
+            pltpu.VMEM((NX, 16, E), BF16),
+            pltpu.VMEM((NX, 16, 128), jnp.int32),
+            pltpu.VMEM((NY, 16, E), BF16),
+            pltpu.VMEM((NY, 16, E), BF16),
+            pltpu.VMEM((NX, 16, E), BF16),
+            pltpu.VMEM((NX, 16, E), BF16),
+            pltpu.VMEM((16, E), F32),
+            pltpu.VMEM((NZ, 4, E), F32),
+            pltpu.VMEM((NZ, 4, E), F32),
+            pltpu.VMEM((NM, 16, E), BF16),
+            pltpu.SemaphoreType.DMA((8, 8)),
+            pltpu.SemaphoreType.DMA((8, 8)),
+        ],
+        compiler_params=pltpu.CompilerParams(
+            collective_id=0, has_side_effects=True, vmem_limit_bytes=48 * 1024 * 1024
+        ),
+    )(
+        raw,
+        captions,
+        jnp.broadcast_to(positives[:, None], (16, 128)),
+        jnp.stack([logit_scale, logit_bias]),
+    )
 
 
 def on_device(
@@ -68,41 +295,7 @@
     raw = lax.psum(
         jnp.dot(pooled, projection, preferred_element_type=jnp.float32).astype(jnp.bfloat16), "mp"
     ).astype(jnp.float32)
-    video_embed = raw * lax.rsqrt(jnp.sum(raw * raw, axis=-1, keepdims=True) + epsilon)
-    video_unit = video_embed.astype(jnp.bfloat16)
-    caption_values = captions.astype(jnp.float32)
-    text_unit = (
-        caption_values
-        * lax.rsqrt(jnp.sum(caption_values * caption_values, axis=-1, keepdims=True) + epsilon)
-    ).astype(jnp.bfloat16)
-    text_column = lax.all_gather(text_unit, "dp", axis=0, tiled=True)
-    caption_rows = captions.shape[0]
-    dp_count = lax.axis_size("dp")
-    mp_count = lax.axis_size("mp")
-    column_pos = jnp.arange(dp_count * caption_rows, dtype=jnp.int32)
-    owner_dp = column_pos // caption_rows
-    within_row = column_pos % caption_rows
-    column_ids = (owner_dp * mp_count + lax.axis_index("mp")) * caption_rows + within_row
-    labels = jnp.where(
-        column_ids[None, :] == positives[:, None], jnp.float32(1.0), jnp.float32(-1.0)
-    )
-    logits = (
-        logit_scale
-        * lax.dot_general(
-            video_unit, text_column, (((1,), (1,)), ((), ())), preferred_element_type=jnp.float32
-        )
-        + logit_bias
-    )
-    pair_weights = (-labels * jax.nn.sigmoid(-labels * logits)).astype(jnp.bfloat16)
-    video_part = logit_scale * jnp.dot(
-        pair_weights, text_column, preferred_element_type=jnp.float32
-    )
-    text_part = logit_scale * lax.dot_general(
-        pair_weights, video_unit, (((0,), (0,)), ((), ())), preferred_element_type=jnp.float32
-    )
-    text_grad = lax.psum_scatter(text_part, "dp", scatter_dimension=0, tiled=True)
-    video_grad = lax.psum(video_part.astype(jnp.bfloat16), "mp").astype(jnp.float32)
-    return (video_embed, video_grad, text_grad)
+    return loss_part(raw, captions, positives, logit_scale, logit_bias)
 
 
 def solution(mesh):

time: 1990 us -> 464 us (0.23)
  waiting for transfers between devices: 1900 us -> 362 us
  Pallas kernels: 0 us -> 34.1 us
    unnamed x7 -> x4, waiting for transfers between devices: 1440 us -> 1.41 us
    all_gather x1 -> x0, waiting for transfers between devices: 100 us -> none  [on_device(): text_column = lax.all_gather(text_unit, 'dp', axis=0, tiled=True)]
    pallas_call x0 -> x1, Pallas kernels: none -> 34.1 us  [loss_part(): pl.pallas_call(loss_kernel, out_shape=(jax.ShapeDtypeStruct((16, E), F32)...]
  transfers between devices with their start and end apart: 6 -> 4, of which waited for: 6 -> 4; matrix products, arithmetic and copies ran while one was open for 2% -> 4% of each run, Pallas kernels for 0% -> 0%
where the time goes in v1:
time: 464 us; the launch traced here: 463 us
  waiting for transfers between devices  362 us (78%)
  Pallas kernels  34.1 us (7%)
  local copies, waits for them, and re-layouts  20.1 us (4%)
  between operations  15.2 us (3%)
  other arithmetic  11.8 us (3%)
  blocking collectives  10.3 us (2%)
  matrix products  9.59 us (2%)
    all_gather x1, waiting for transfers between devices, on_device(): lax.all_gather(down_weight, 'dp', axis=0, tiled=True)  124 us
    all_gather x1, waiting for transfers between devices, on_device(): lax.all_gather(up_weight, 'dp', axis=0, tiled=True)  117 us
    all_gather x1, waiting for transfers between devices, on_device(): gathered = lax.all_gather(frames, 'mp', axis=2, tiled=True)  67.5 us
    psum x1, waiting for transfers between devices, on_device(): lax.psum(partial_value.astype(jnp.bfloat16), 'mp').astype(jnp.float32)  51.6 us
    pallas_call x1, Pallas kernels, loss_part(): pl.pallas_call(loss_kernel, out_shape=(jax.ShapeDtypeStruct((16, E), F32)...  34.1 us
    unnamed x26, local copies, waits for them, and re-layouts  12.1 us
    psum x1, blocking collectives, on_device(): lax.psum(jnp.dot(pooled, projection, preferred_element_type=jnp.float32)....  10.3 us
    dot_general x1, matrix products, on_device(): lax.dot_general(hidden, lax.all_gather(down_weight, 'dp', axis=0, tiled=T...  9.34 us
  transfers between devices with their start and end apart: 4, of which 4 were waited for; matrix products, arithmetic and copies ran while one was open for 4% of the time, Pallas kernels for 0%

profile of v1, /device:TPU:6, one launch (start us, length us, event | category | flops | bytes accessed | tf_op | source)
XLA Modules:
  0.0 463.1 jit_solution(3222431633031459503)
XLA Ops:
  7.2 0.0 all-gather.6.cloned.1.call-start
  7.2 2.8 copy.18
  10.0 0.0 all-gather.6.cloned.1.call-update
  10.0 0.0 all-gather.8.cloned.1.call-start
  10.1 0.7 all-gather.8.cloned.1.call-update
  10.8 0.0 all-gather.10.cloned.1.call-start
  10.8 0.7 all-gather.10.cloned.1.call-update
  11.5 0.0 all-reduce.2.cloned.1.call-start
  11.5 67.5 %all-gather.6.cloned.1.call-done = bf16[16,32,1408]{1,0,2:T(8,128)(2,1)} async-done(((bf16[16,32,352]{1,0,2:T(8,128)(2,1)}), bf16[16,32,1408]{1,0,2:T(8,128)(2,1)}) %all-gather.6.cloned.1.call-update) | async-done | bytes 1441808 | tf_op jit(solution)/shard_map/all_gather | solution.py:258
  79.1 4.7 %convert_reduce_fusion = (f32[16,32]{1,0:T(8,128)S(1)}, f32[16,32]{1,0:T(8,128)S(1)}) fusion(bf16[16,32,1408]{1,0,2:T(8,128)(2,1)} %all-gather.6.cloned.1.call-done), kind=kLoop, calls=%fused_computation.1 | loop fusion | flops 2882560 | bytes 1445888 | tf_op jit(solution)/shard_map/reduce_sum | solution.py:260
  83.8 0.1 div.25
  83.9 0.1 div.27
  83.9 7.8 %copy.19 = f32[16,32,1408]{2,1,0:T(8,128)} copy(bf16[16,32,1408]{1,0,2:T(8,128)(2,1)} %all-gather.6.cloned.1.call-done) | data formatting | bytes 4325376 | tf_op jit(solution)/shard_map/convert_element_type | solution.py:259
  91.8 3.5 fusion.3
  95.2 116.9 %all-gather.8.cloned.1.call-done = bf16[128,11,768]{2,1,0:T(8,128)(2,1)} async-done(((bf16[1,11,768]{2,1,0:T(8,128)(2,1)}), bf16[128,11,768]{2,1,0:T(8,128)(2,1)}) %all-gather.8.cloned.1.call-update) | async-done | bytes 2162704 | tf_op jit(solution)/shard_map/all_gather | solution.py:268
  212.1 3.0 reshape.96
  215.1 124.4 %all-gather.10.cloned.1.call-done = bf16[128,11,768]{2,1,0:T(8,128)(2,1)} async-done(((bf16[1,11,768]{2,1,0:T(8,128)(2,1)}), bf16[128,11,768]{2,1,0:T(8,128)(2,1)}) %all-gather.10.cloned.1.call-update) | async-done | bytes 2162704 | tf_op jit(solution)/shard_map/all_gather | solution.py:274
  339.6 4.4 reshape.98
  344.0 9.3 %convolution_convert_fusion = bf16[512,1408]{1,0:T(8,128)(2,1)} fusion(bf16[1408,768]{1,0:T(8,128)(2,1)} %reshape.98, bf16[512,1408]{1,0:T(8,128)(2,1)} %fusion.3, bf16[1408,768]{1,0:T(8,128)(2,1)S(1)} %reshape.96, f32[768]{0:T(1024)S(1)} %copy-done.9), kind=kOutput, calls=%fused_computation.2 | convolution fusion | flops 2241265664 | bytes 7212032 | tf_op jit(solution)/shard_map/dot_general | solution.py:272
  353.3 0.0 all-reduce.2.cloned.1.call-update
  354.7 0.1 pad_maximum_fusion.scalars_ref
  354.7 0.1 fusion.50
  354.8 51.6 %all-reduce.2.cloned.1.call-done = bf16[512,1408]{1,0:T(8,128)(2,1)} async-done(((bf16[512,1408]{1,0:T(8,128)(2,1)}), bf16[512,1408]{1,0:T(8,128)(2,1)}) %all-reduce.2.cloned.1.call-update) | async-done | bytes 1441808 | tf_op jit(solution)/shard_map/psum | solution.py:279
  406.4 2.9 fusion.81
  409.4 0.5 multiply_reduce_fusion.2
  409.9 0.3 convolution_convert_fusion.1
  410.2 10.3 %psum.15 = bf16[16,1024]{1,0:T(8,128)(2,1)S(1)} all-reduce(bf16[16,1024]{1,0:T(8,128)(2,1)S(1)} %convolution_convert_fusion.1), channel_id=1, replica_groups=mesh['dp'=128,'mp'=4] {'mp'}, use_global_device_ids=true, to_apply=%region_6.0 | all-reduce | flops 16384 | bytes 65536 | tf_op jit(solution)/shard_map/psum | solution.py:295
  420.5 0.1 broadcast_in_dim.2.positives_ref
  420.6 34.1 %shard_map.166 = (f32[16,1024]{1,0:T(8,128)S(1)}, f32[16,1024]{1,0:T(8,128)S(1)}, f32[4,1024]{1,0:T(4,128)S(1)}) custom-call(f32[16,1024]{1,0:T(8,128)S(1)} %convert_element_type.53.raw_ref, bf16[4,1024]{1,0:T(4,128)(2,1)S(1)} %copy-done.1, s32[16,128]{1,0:T(8,128)S(1)} %broadcast_in_dim.2.positives_ref, f32[2]{0:T(128)S(1)} %pad_maximum_fusion.scalars_ref), custom_call_target="tpu_custom_call" | custom-call | tf_op jit(solution)/shard_map/pallas_call | solution.py:202
  454.7 0.6 copy.26
  455.3 0.6 copy.27
  456.0 0.6 copy.28
  (25 shorter events, 0.1 us)
Async XLA Ops:
  7.2 402.7 %copy-start = (bf16[352,1024]{1,0:T(8,128)(2,1)S(1)}, bf16[352,1024]{1,0:T(8,128)(2,1)}, u32[]{:S(2)}) copy-start(bf16[352,1024]{1,0:T(8,128)(2,1)} %param.25) | copy-start | bytes 2162692
  7.2 71.9 %all-gather.6.cloned.1.call-start = ((), (), s32[]{:S(2)}) async-start(), calls=%async_computation | async-start | bytes 7208960 | tf_op jit(solution)/shard_map/all_gather | solution.py:258
  10.0 202.1 %all-gather.8.cloned.1.call-start = ((), (), s32[]{:S(2)}) async-start(), calls=%async_computation.2 | async-start | bytes 3170304 | tf_op jit(solution)/shard_map/all_gather | solution.py:268
  10.8 328.8 %all-gather.10.cloned.1.call-start = ((), (), s32[]{:S(2)}) async-start(), calls=%async_computation.3 | async-start | bytes 3170304 | tf_op jit(solution)/shard_map/all_gather | solution.py:274
  11.5 394.9 %all-reduce.2.cloned.1.call-start = ((), (), s32[]{:S(2)}) async-start(), calls=%async_computation.1 | async-start | bytes 2883584 | tf_op jit(solution)/shard_map/psum | solution.py:279
  83.9 7.8 %copy-start.2 = (f32[1408]{0:T(1024)S(1)}, f32[1408]{0:T(1024)}, u32[]{:S(2)}) copy-start(f32[1408]{0:T(1024)} %param.18) | copy-start | bytes 16900
  83.9 7.8 %copy-start.3 = (f32[1408]{0:T(1024)S(1)}, f32[1408]{0:T(1024)}, u32[]{:S(2)}) copy-start(f32[1408]{0:T(1024)} %param.17) | copy-start | bytes 16900
  215.1 128.9 %copy-start.9 = (f32[768]{0:T(1024)S(1)}, f32[768]{0:T(1024)}, u32[]{:S(2)}) copy-start(f32[768]{0:T(1024)} %param.20) | copy-start | bytes 9220
  344.0 9.4 %copy-start.7 = (s32[16]{0:T(128)S(1)}, s32[16]{0:T(128)}, u32[]{:S(2)}) copy-start(s32[16]{0:T(128)} %param.16) | copy-start | bytes 196
  344.0 62.4 %copy-start.4 = (f32[1408]{0:T(1024)S(1)}, f32[1408]{0:T(1024)}, u32[]{:S(2)}) copy-start(f32[1408]{0:T(1024)} %param.22) | copy-start | bytes 16900
  354.8 54.5 %copy-start.5 = (f32[352]{0:T(512)S(1)}, f32[352]{0:T(512)}, u32[]{:S(2)}) copy-start(f32[352]{0:T(512)} %param.24) | copy-start | bytes 4228
  354.8 54.5 %copy-start.6 = (f32[352]{0:T(512)S(1)}, f32[352]{0:T(512)}, u32[]{:S(2)}) copy-start(f32[352]{0:T(512)} %param.23) | copy-start | bytes 4228
  409.3 11.2 %copy-start.8 = (s32[16]{0:T(128)S(1)}, s32[16]{0:T(128)}, u32[]{:S(2)}) copy-start(s32[16]{0:T(128)} %param.27) | copy-start | bytes 196
  409.3 11.2 %copy-start.1 = (bf16[4,1024]{1,0:T(4,128)(2,1)S(1)}, bf16[4,1024]{1,0:T(4,128)(2,1)}, u32[]{:S(2)}) copy-start(bf16[4,1024]{1,0:T(4,128)(2,1)} %captions_ref.1) | copy-start | bytes 24580
Sparse Core Ops, SparseCore 0:
  10.1 68.9 all-gather.5
  83.6 128.4 all-gather.7
  216.7 122.8 all-gather.9
  353.5 52.9 all-reduce.1

commit v2 on v1

v2 whole, which is shorter than its diff:
```python
import jax
import jax.numpy as jnp
import numpy as np
from jax import lax
from jax.experimental import pallas as pl
from jax.experimental.pallas import tpu as pltpu
from jax.sharding import PartitionSpec as P

D = 1408
E = 1024
NY, NZ, NX, NM = 8, 4, 4, 4
MESH = pl.DeviceIdType.MESH
epsilon = 1e-06
F32 = jnp.float32
BF16 = jnp.bfloat16


def position():
    dp = lax.axis_index("dp")
    mp = lax.axis_index("mp")
    return dp // (NZ * NX), (dp // NX) % NZ, dp % NX, mp


def device(y, z, x, m):
    return ((y * NZ + z) * NX + x, m)


def peer_at(axis, step):
    y, z, x, m = position()
    if axis == "y":
        place = (y + step) % NY
        return device(place, z, x, m), place
    if axis == "z":
        place = (z + step) % NZ
        return device(y, place, x, m), place
    if axis == "x":
        place = (x + step) % NX
        return device(y, z, place, m), place
    place = (m + step) % NM
    return device(y, z, x, place), place


SIZES = {"y": NY, "z": NZ, "x": NX, "m": NM}


def greet():
    barrier = pltpu.get_barrier_semaphore()
    total = 0
    for axis, size in SIZES.items():
        for step in range(1, size):
            target, _ = peer_at(axis, step)
            pl.semaphore_signal(barrier, inc=1, device_id=target, device_id_type=MESH)
            total += 1
    pl.semaphore_wait(barrier, total)


class Links:
    def __init__(self, send_sems, recv_sems):
        self.send_sems, self.recv_sems = send_sems, recv_sems
        self.rows = 0
        self.sent = []

    def row(self):
        self.rows += 1
        return self.rows - 1

    def make(self, source, slot, row, send_index, recv_index, target):
        return pltpu.make_async_remote_copy(
            src_ref=source,
            dst_ref=slot,
            send_sem=self.send_sems.at[row, send_index],
            recv_sem=self.recv_sems.at[row, recv_index],
            device_id=target,
            device_id_type=MESH,
        )

    def send(self, source, slot, row, send_index, recv_index, target):
        copy = self.make(source, slot, row, send_index, recv_index, target)
        copy.start()
        self.sent.append(copy)

    def arrive(self, slot, row, recv_index, target):
        self.make(slot, slot, row, 0, recv_index, target).wait_recv()

    def finish(self):
        for copy in self.sent:
            copy.wait_send()


class Exchange:
    def __init__(self, links, axis, source, slots):
        self.links, self.axis, self.slots = links, axis, slots
        self.row = links.row()
        y, z, x, m = position()
        own = {"y": y, "z": z, "x": x, "m": m}[axis]
        for step in range(1, SIZES[axis]):
            target, place = peer_at(axis, step)
            links.send(source(place), slots.at[own], self.row, step, own, target)

    def wait(self):
        for step in range(1, SIZES[self.axis]):
            target, place = peer_at(self.axis, step)
            self.links.arrive(self.slots.at[place], self.row, place, target)


def one_hot(hit):
    return jnp.where(hit, F32(1.0), F32(0.0)).astype(BF16)


def dot(a, b):
    return jnp.dot(a, b, preferred_element_type=F32)


def dot_t(a, b):
    return lax.dot_general(a, b, (((1,), (1,)), ((), ())), preferred_element_type=F32)


def iota(shape, dim):
    return lax.broadcasted_iota(jnp.int32, shape, dim)


def gelu(v):
    return 0.5 * v * (1.0 + lax.erf(v * F32(0.7071067811865476)))


def step_kernel(
    frames_ref,
    weight_ref,
    up_shard_ref,
    down_shard_ref,
    feature_ref,
    norm_ref,
    up_bias_ref,
    final_ref,
    projection_ref,
    captions_ref,
    positives_ref,
    scalars_ref,
    embed_ref,
    video_ref,
    text_ref,
    shard_z,
    up_x,
    up_y,
    down_x,
    frames_all,
    normed,
    order,
    bias_rows,
    resid,
    chip_out,
    chip_in,
    pair_out,
    pair_in,
    pool_rows,
    pool_out,
    pool_in,
    pool_all,
    raw_in,
    text_z,
    text_rows,
    text_y,
    video_x,
    where_x,
    text_out,
    text_in,
    video_out,
    video_in,
    text_sum,
    text_part,
    text_last,
    mp_in,
    send_sems,
    recv_sems,
):
    y, z, x, m = position()
    half, core = m // 2, m % 2
    chip_mate = half * 2 + (1 - core)
    pair_mate = (1 - half) * 2 + core
    far_mate = (1 - half) * 2 + (1 - core)
    chip_id = device(y, z, x, chip_mate)
    pair_id = device(y, z, x, pair_mate)
    up_id, up_from = peer_at("y", 1)
    down_id, down_from = peer_at("y", NY - 1)
    right_id, right = peer_at("x", 1)
    left_id, left = peer_at("x", NX - 1)
    across = (x + 2) % NX
    scale = scalars_ref[0]
    bias = scalars_ref[1]
    links = Links(send_sems, recv_sems)
    greet()

    shard_z[z] = jnp.zeros((2, 16, 768), BF16)
    shard_z[z, 0, 0:11, :] = up_shard_ref[...]
    shard_z[z, 1, 0:11, :] = down_shard_ref[...]
    gather_shards = Exchange(links, "z", lambda place: shard_z.at[z], shard_z)
    frames_row = links.row()
    links.send(frames_ref, frames_all.at[m], frames_row, 0, 0, chip_id)
    caption_values = captions_ref[...].astype(F32)
    text_z[z] = caption_values * lax.rsqrt(
        jnp.sum(caption_values * caption_values, axis=-1, keepdims=True) + epsilon
    )
    gather_text_z = Exchange(links, "z", lambda place: text_z.at[z], text_z)
    where_x[x] = positives_ref[...]
    gather_where = Exchange(links, "x", lambda place: where_x.at[x], where_x)
    frames_all[m] = frames_ref[...]

    slot_of = iota((48, 64), 1)
    target_row = lax.shift_right_logical(slot_of, 4) * 11 + lax.bitwise_and(slot_of, 15)
    pack_z = one_hot((iota((48, 64), 0) == target_row) & (lax.bitwise_and(slot_of, 15) < 11))
    gather_shards.wait()
    up_x[x] = dot(pack_z, shard_z[:, 0].reshape(64, 768)).astype(BF16)
    gather_up_x = Exchange(links, "x", lambda place: up_x.at[x], up_x)
    down_x[x, y] = dot(pack_z, shard_z[:, 1].reshape(64, 768)).astype(BF16)

    offsets = [0, -1, 1, -2, 2, -3, 3, -4]
    ring_row, from_left, from_right, from_across = links.row(), links.row(), links.row(), links.row()
    send_right, send_left = from_left, from_right

    def block_y(k):
        return (y + offsets[k] + NY) % NY

    def pass_down(k):
        block = down_x.at[x, block_y(k)]
        if k == 0 or (k % 2 == 1 and k < 7):
            following = 1 if k == 0 else k + 2
            links.send(block, block, ring_row, following, following, up_id)
        if k == 0 or (k % 2 == 0 and k < 6):
            links.send(block, block, ring_row, k + 2, k + 2, down_id)
        links.send(block, block, send_right, k, k, right_id)
        links.send(block, block, send_left, k, k, left_id)

    def take_down(k):
        links.arrive(down_x.at[x, block_y(k)], ring_row, k, up_id)
        pass_down(k)

    def take_side(k):
        left_block = down_x.at[left, block_y(k)]
        right_block = down_x.at[right, block_y(k)]
        links.arrive(left_block, from_left, k, left_id)
        if k % 2 == 0:
            links.send(left_block, left_block, from_across, k, k, right_id)
        links.arrive(right_block, from_right, k, right_id)
        if k % 2 == 1:
            links.send(right_block, right_block, from_across, k, k, left_id)

    pass_down(0)
    links.send(frames_ref, frames_all.at[m], frames_row, 1, 1, pair_id)

    slot_of = iota((176, 192), 1)
    from_x = (slot_of >= 48).astype(jnp.int32) + (slot_of >= 96).astype(jnp.int32) + (
        slot_of >= 144
    ).astype(jnp.int32)
    inside = slot_of - 48 * from_x
    from_z = (inside >= 11).astype(jnp.int32) + (inside >= 22).astype(jnp.int32) + (
        inside >= 33
    ).astype(jnp.int32)
    target_row = (from_z * 4 + from_x) * 11 + inside - 11 * from_z
    pack_x = one_hot((iota((176, 192), 0) == target_row) & (inside < 44))
    gather_up_x.wait()
    up_y[y] = dot(pack_x, up_x[...].reshape(192, 768)).astype(BF16)
    up_right, up_left = links.row(), links.row()

    def ring_part(ref, block, step, rightwards):
        if step < 4:
            return ref.at[block]
        return ref.at[block, 0:96, :] if rightwards else ref.at[block, 96:176, :]

    def pass_up(step):
        ahead = ring_part(up_y, (y - (step - 1) + NY) % NY, step, True)
        links.send(ahead, ahead, up_right, step, step, up_id)
        behind = ring_part(up_y, (y + (step - 1)) % NY, step, False)
        links.send(behind, behind, up_left, step, step, down_id)

    def take_up(step):
        links.arrive(ring_part(up_y, (y - step + NY) % NY, step, True), up_right, step, up_id)
        links.arrive(ring_part(up_y, (y + step) % NY, step, False), up_left, step, down_id)
        if step < 4:
            pass_up(step + 1)

    pass_up(1)
    take_down(1)
    take_down(2)
    take_side(0)
    gather_text_z.wait()
    for slot in range(NZ):
        text_rows[4 * slot : 4 * slot + 4, :] = text_z[slot]
    text_y[y] = text_rows[...].astype(BF16)
    take_down(3)
    take_down(4)
    take_side(1)
    take_side(2)
    take_up(1)
    take_down(5)
    take_down(6)
    take_side(3)
    links.arrive(frames_all.at[pair_mate], frames_row, 1, pair_id)
    links.send(frames_all.at[pair_mate], frames_all.at[pair_mate], frames_row, 2, 2, chip_id)
    links.arrive(frames_all.at[chip_mate], frames_row, 0, chip_id)
    take_down(7)
    take_side(4)
    for quarter in range(NM):
        hit = iota((352, 1536), 0) + 352 * quarter == feature_ref[...]
        order[quarter] = one_hot(hit)
    take_side(5)
    take_up(2)
    links.arrive(frames_all.at[far_mate], frames_row, 2, chip_id)

    def normalise(step, carry):
        rows = pl.ds(pl.multiple_of(step * 32, 32), 32)
        values = [frames_all[quarter, rows, :].astype(F32) for quarter in range(NM)]
        total = sum(jnp.sum(v, axis=-1, keepdims=True) for v in values)
        squares = sum(jnp.sum(v * v, axis=-1, keepdims=True) for v in values)
        mean = total * F32(1.0 / D)
        factor = lax.rsqrt(squares * F32(1.0 / D) - mean * mean + epsilon)
        for quarter in range(NM):
            normed[quarter, rows, :] = (
                (values[quarter] - mean) * factor * norm_ref[quarter, 0:1, :]
                + norm_ref[quarter, 1:2, :]
            ).astype(BF16)
        return carry

    lax.fori_loop(0, 8, normalise, 0)
    take_side(6)
    take_side(7)
    lax.fori_loop(8, 16, normalise, 0)
    take_up(3)
    gather_text_y = Exchange(links, "y", lambda place: text_y.at[y], text_y)

    def rows_of(place):
        return pl.ds(pl.multiple_of(place * 128, 128), 128)

    own = jnp.zeros((128, 1536), F32)
    own_bias = jnp.zeros((16, 1536), F32)
    for quarter in range(NM):
        own += dot(frames_all[quarter, rows_of(m), :], order[quarter])
        bias_part = norm_ref[quarter, 2:3, :]
        bias_rows[...] = jnp.zeros((16, 352), F32)
        for piece in range(3):
            rounded = bias_part.astype(BF16).astype(F32)
            bias_rows[piece : piece + 1, :] = rounded
            bias_part = bias_part - rounded
        own_bias += dot(bias_rows[...].astype(BF16), order[quarter])
    resid[...] = own + jnp.sum(own_bias, axis=0, keepdims=True)
    take_up(4)
    for k in range(NY):
        links.arrive(down_x.at[across, block_y(k)], from_across, k, right_id)

    def hidden_of(place):
        total = jnp.broadcast_to(up_bias_ref[...], (128, 768))
        for quarter in range(NM):
            total += dot(
                normed[quarter, rows_of(place), :],
                up_y[2 * quarter : 2 * quarter + 2].reshape(352, 768),
            )
        return gelu(total).astype(BF16)

    def partial_sums(hidden, block):
        return dot_t(hidden, down_x[block].reshape(384, 768))

    chip_row, pair_row = links.row(), links.row()
    hidden = hidden_of(far_mate)
    for block in range(NX):
        chip_out[0, :, 384 * block : 384 * block + 384] = partial_sums(hidden, block).astype(BF16)
    links.send(chip_out.at[0], chip_in.at[0], chip_row, 0, 0, chip_id)
    hidden = hidden_of(pair_mate)
    links.arrive(chip_in.at[0], chip_row, 0, chip_id)
    for block in range(NX):
        lanes = slice(384 * block, 384 * block + 384)
        pair_out[:, lanes] = (
            partial_sums(hidden, block) + chip_in[0, :, lanes].astype(F32)
        ).astype(BF16)
    links.send(pair_out, pair_in, pair_row, 0, 0, pair_id)
    hidden = hidden_of(chip_mate)
    for block in range(NX):
        chip_out[1, :, 384 * block : 384 * block + 384] = partial_sums(hidden, block).astype(BF16)
    links.send(chip_out.at[1], chip_in.at[1], chip_row, 1, 1, chip_id)
    hidden = hidden_of(m)
    links.arrive(chip_in.at[1], chip_row, 1, chip_id)
    for block in range(NX):
        lanes = slice(384 * block, 384 * block + 384)
        resid[:, lanes] += partial_sums(hidden, block) + chip_in[1, :, lanes].astype(F32)
    gather_text_y.wait()
    gather_where.wait()
    links.arrive(pair_in, pair_row, 0, pair_id)

    pool_rows[...] = jnp.zeros((16, 1536), F32)
    for clip in range(4):
        rows = slice(32 * clip, 32 * clip + 32)
        values = resid[rows, :] + pair_in[rows, :].astype(F32)
        mean = jnp.sum(values, axis=-1, keepdims=True) * F32(1.0 / D)
        square = jnp.sum(values * values, axis=-1, keepdims=True) * F32(1.0 / D)
        factor = lax.rsqrt(square - mean * mean + epsilon)
        weight = weight_ref[pl.ds(pl.multiple_of(m * 128 + 32 * clip, 32), 32), 0:1]
        mixed = jnp.sum((values - mean) * (factor * weight), axis=0, keepdims=True)
        rounded = mixed.astype(BF16).astype(F32)
        pool_rows[clip : clip + 1, :] = rounded
        pool_rows[clip + 4 : clip + 5, :] = mixed - rounded
    packed = pool_rows[...].astype(BF16)
    for quarter in range(NM):
        natural = dot_t(packed, order[quarter])
        pool_out[quarter] = natural[0:4, :] + natural[4:8, :]
    pool_in[m] = pool_out[m]
    share_pool = Exchange(links, "m", lambda place: pool_out.at[place], pool_in)
    share_pool.wait()
    for slot in range(NM):
        pool_all[4 * slot : 4 * slot + 4, :] = pool_in[slot]
    pooled = (pool_all[...] * final_ref[0:1, :] + final_ref[1:2, :]).astype(BF16)
    raw_in[m] = dot(pooled, projection_ref[...]).astype(BF16)
    share_raw = Exchange(links, "m", lambda place: raw_in.at[m], raw_in)
    share_raw.wait()
    raw = raw_in[0].astype(F32)
    for slot in range(1, NM):
        raw += raw_in[slot].astype(F32)

    embed = raw * lax.rsqrt(jnp.sum(raw * raw, axis=-1, keepdims=True) + epsilon)
    embed_ref[...] = embed
    video_x[x] = embed.astype(BF16)
    gather_video = Exchange(links, "x", lambda place: video_x.at[x], video_x)
    column = iota((NX * 16, NY * 16), 1)
    owner = lax.shift_right_logical(column, 2)
    ids = (((owner * 4) + x) * 4 + m) * 4 + lax.bitwise_and(column, 3)
    labels = jnp.where(ids == where_x[...].reshape(NX * 16, 128), F32(1.0), F32(-1.0))
    text = text_y[...].reshape(NY * 16, E)
    gather_video.wait()
    video = video_x[...].reshape(NX * 16, E)
    logits = scale * dot_t(video, text) + bias
    pair_weights = -labels * lax.logistic(-labels * logits)
    turned = jnp.transpose(pair_weights).astype(BF16)
    text_out[...] = (scale * dot(turned, video)).astype(BF16).reshape(NY, 16, E)
    text_in[y] = text_out[y]
    reduce_text_y = Exchange(links, "y", lambda place: text_out.at[place], text_in)
    video_out[...] = (scale * dot(pair_weights.astype(BF16), text)).astype(BF16).reshape(NX, 16, E)
    video_in[x] = video_out[x]
    reduce_video_x = Exchange(links, "x", lambda place: video_out.at[place], video_in)

    reduce_video_x.wait()
    video_total = video_in[0].astype(F32)
    for slot in range(1, NX):
        video_total += video_in[slot].astype(F32)
    mp_in[m] = video_total.astype(BF16)
    share_video = Exchange(links, "m", lambda place: mp_in.at[m], mp_in)
    reduce_text_y.wait()
    text_total = text_in[0].astype(F32)
    for slot in range(1, NY):
        text_total += text_in[slot].astype(F32)
    text_sum[...] = text_total
    for slot in range(NZ):
        text_part[slot] = text_sum[4 * slot : 4 * slot + 4, :]
    text_last[z] = text_part[z]
    reduce_text_z = Exchange(links, "z", lambda place: text_part.at[place], text_last)
    share_video.wait()
    video_grad = mp_in[0].astype(F32)
    for slot in range(1, NM):
        video_grad += mp_in[slot].astype(F32)
    video_ref[...] = video_grad
    reduce_text_z.wait()
    text_grad = text_last[0]
    for slot in range(1, NZ):
        text_grad += text_last[slot]
    text_ref[...] = text_grad
    links.finish()


def arrival_order():
    feature = np.full((NX, NY, 48), -1, np.int32)
    for x in range(NX):
        for y in range(NY):
            for z in range(NZ):
                first = ((y * NZ + z) * NX + x) * 11
                feature[x, y, 11 * z : 11 * z + 11] = np.arange(first, first + 11)
    return feature.reshape(1, 1536)


def on_device(
    frames,
    frame_counts,
    norm_gain,
    norm_bias,
    up_weight,
    up_bias,
    down_weight,
    down_bias,
    final_gain,
    final_bias,
    projection,
    captions,
    positives,
    logit_scale,
    logit_bias,
):
    slots = jnp.arange(32, dtype=jnp.int32)[None, :]
    counts = frame_counts[:, None]
    weights = jnp.where(slots < counts, 1.0 / counts.astype(F32), 0.0)
    weights = jnp.broadcast_to(weights.reshape(512, 1), (512, 128))
    norm = jnp.stack([part.reshape(4, 352) for part in (norm_gain, norm_bias, down_bias)], axis=1)
    vmem = pl.BlockSpec(memory_space=pltpu.VMEM)
    smem = pl.BlockSpec(memory_space=pltpu.SMEM)
    return pl.pallas_call(
        step_kernel,
        out_shape=(
            jax.ShapeDtypeStruct((16, E), F32),
            jax.ShapeDtypeStruct((16, E), F32),
            jax.ShapeDtypeStruct((4, E), F32),
        ),
        in_specs=[vmem] * 11 + [smem],
        out_specs=(vmem, vmem, vmem),
        scratch_shapes=[
            pltpu.VMEM((NZ, 2, 16, 768), BF16),
            pltpu.VMEM((NX, 48, 768), BF16),
            pltpu.VMEM((NY, 176, 768), BF16),
            pltpu.VMEM((NX, NY, 48, 768), BF16),
            pltpu.VMEM((NM, 512, 352), BF16),
            pltpu.VMEM((NM, 512, 352), BF16),
            pltpu.VMEM((NM, 352, 1536), BF16),
            pltpu.VMEM((16, 352), F32),
            pltpu.VMEM((128, 1536), F32),
            pltpu.VMEM((2, 128, 1536), BF16),
            pltpu.VMEM((2, 128, 1536), BF16),
            pltpu.VMEM((128, 1536), BF16),
            pltpu.VMEM((128, 1536), BF16),
            pltpu.VMEM((16, 1536), F32),
            pltpu.VMEM((NM, 4, 352), F32),
            pltpu.VMEM((NM, 4, 352), F32),
            pltpu.VMEM((16, 352), F32),
            pltpu.VMEM((NM, 16, E), BF16),
            pltpu.VMEM((NZ, 4, E), F32),
            pltpu.VMEM((16, E), F32),
            pltpu.VMEM((NY, 16, E), BF16),
            pltpu.VMEM((NX, 16, E), BF16),
            pltpu.VMEM((NX, 16, 128), jnp.int32),
            pltpu.VMEM((NY, 16, E), BF16),
            pltpu.VMEM((NY, 16, E), BF16),
            pltpu.VMEM((NX, 16, E), BF16),
            pltpu.VMEM((NX, 16, E), BF16),
            pltpu.VMEM((16, E), F32),
            pltpu.VMEM((NZ, 4, E), F32),
            pltpu.VMEM((NZ, 4, E), F32),
            pltpu.VMEM((NM, 16, E), BF16),
            pltpu.SemaphoreType.DMA((24, 8)),
            pltpu.SemaphoreType.DMA((24, 8)),
        ],
        compiler_params=pltpu.CompilerParams(
            collective_id=0, has_side_effects=True, vmem_limit_bytes=56 * 1024 * 1024
        ),
    )(
        frames.reshape(512, 352),
        weights,
        up_weight,
        down_weight,
        jnp.asarray(arrival_order()),
        norm,
        up_bias.reshape(1, 768),
        jnp.stack([final_gain, final_bias]),
        projection,
        captions,
        jnp.broadcast_to(positives[:, None], (16, 128)),
        jnp.stack([logit_scale, logit_bias]),
    )


def solution(mesh):
    return jax.shard_map(
        on_device,
        mesh=mesh,
        in_specs=(
            P("dp", None, "mp"),
            P("dp"),
            P(),
            P(),
            P("dp", "mp"),
            P("mp"),
            P("dp", "mp"),
            P(),
            P("mp"),
            P("mp"),
            P("mp", None),
            P(("dp", "mp"), None),
            P("dp"),
            P(),
            P(),
        ),
        out_specs=(P("dp", None), P("dp", None), P(("dp", "mp"), None)),
        check_vma=False,
    )
```

time: 464 us -> 119 us (0.26)
  waiting for transfers between devices: 362 us -> 0 us
  Pallas kernels: 34.1 us -> 105 us
  between operations: 15.2 us -> 1.97 us
  local copies, waits for them, and re-layouts: 20.1 us -> 7.81 us
  blocking collectives: 10.3 us -> 0 us
  other arithmetic: 11.8 us -> 1.96 us
  matrix products: 9.59 us -> 0 us
    all_gather x3 -> x0, waiting for transfers between devices: 309 us -> none  [the longest x1 124 us: on_device(): lax.all_gather(down_weight, 'dp', axis=0, tiled=True)]
    pallas_call x1, Pallas kernels: 34.1 us -> 105 us  [on_device(): pl.pallas_call(step_kernel, out_shape=(jax.ShapeDtypeStruct((16, E), F32)...]
    psum x1 -> x0, waiting for transfers between devices: 51.6 us -> none  [on_device(): lax.psum(partial_value.astype(jnp.bfloat16), 'mp').astype(jnp.float32)]
    psum x1 -> x0, blocking collectives: 10.3 us -> none  [on_device(): lax.psum(jnp.dot(pooled, projection, preferred_element_type=jnp.float32)....]
    dot_general x2 -> x0, matrix products: 9.59 us -> none  [the longest x1 9.34 us: on_device(): lax.dot_general(hidden, lax.all_gather(down_weight, 'dp', axis=0, tiled=T...]
    reduce_sum x3 -> x0, other arithmetic: 8.12 us -> none  [the longest x1 4.69 us: on_device(): row_mean = jnp.mean(frame_rows, axis=-1, keepdims=True)]
    convert_element_type x1 -> x0, local copies, waits for them, and re-layouts: 7.8 us -> none  [on_device(): frame_rows = gathered.reshape(row_count, D).astype(jnp.float32)]
    unnamed x26 -> x23, local copies, waits for them, and re-layouts: 12.1 us -> 5.38 us
  transfers between devices with their start and end apart: 4 -> 0, of which waited for: 4 -> 0; matrix products, arithmetic and copies ran while one was open for 4% -> 0% of each run, Pallas kernels for 0% -> 0%
where the time goes in v2:
time: 119 us; the launch traced here: 117 us
  Pallas kernels  105 us (88%)
  local copies, waits for them, and re-layouts  7.81 us (7%)
  between operations  1.97 us (2%)
  other arithmetic  1.96 us (2%)
    pallas_call x1, Pallas kernels, on_device(): pl.pallas_call(step_kernel, out_shape=(jax.ShapeDtypeStruct((16, E), F32)...  105 us
    unnamed x23, local copies, waits for them, and re-layouts  5.38 us

profile of v2, /device:TPU:6, one launch (start us, length us, event | category | flops | bytes accessed | tf_op | source)
XLA Modules:
  0.0 117.2 jit_solution(4513587690620373352)
XLA Ops:
  1.9 0.0 copy-start.8
  1.9 0.7 pad_maximum_fusion.2.scalars_ref
  2.6 0.0 copy-start.6
  2.6 0.0 copy-done.8
  2.6 0.0 copy-start.7
  2.6 0.7 copy-done.6
  3.3 0.0 copy-start.5
  3.3 0.0 copy-done.7
  3.3 0.0 copy-start.2
  3.3 0.6 pad_maximum_fusion.1.final_ref
  3.9 0.1 copy-done.5
  4.0 0.6 reshape.42.up_bias_ref
  4.5 0.0 copy-done.2
  4.5 0.0 copy-start.3
  4.5 0.1 stack_reshape.9
  4.6 0.6 copy-done.3
  5.2 0.1 stack_reshape.10
  5.3 0.6 copy-done.4
  5.9 0.1 stack_reshape.11
  6.0 0.6 pad_maximum_fusion.norm_ref
  6.6 0.1 fusion
  6.7 0.1 select_n.12
  6.8 0.6 copy-done.9
  7.4 0.7 broadcast_in_dim.28.positives_ref
  8.0 0.8 broadcast_in_dim.27.weight_ref
  8.9 105.4 %shard_map.175 = (f32[16,1024]{1,0:T(8,128)}, f32[16,1024]{1,0:T(8,128)}, f32[4,1024]{1,0:T(4,128)}) custom-call(bf16[512,352]{1,0:T(8,128)(2,1)} %bitcast.5, f32[512,128]{1,0:T(8,128)} %broadcast_in_dim.27.weight_ref, bf16[11,768]{1,0:T(8,128)(2,1)} %up_shard_ref.1, bf16[11,768]{1,0:T(8,128)(2,1)} %down_shard_ref.1, s32[1,1536]{1,0:T(1,128)} %constant.6.clone.feature_ref, ...), custom_call_target="tpu_custom_call" | custom-call | tf_op jit(solution)/shard_map/pallas_call | solution.py:499
  114.3 0.0 copy-start
  114.3 1.5 %copy.24 = f32[16,1024]{1,0:T(8,128)} copy(f32[16,1024]{1,0:T(8,128)} %get-tuple-element.6) | data formatting | bytes 131072
  115.8 0.0 copy-done
  115.8 0.6 copy.25
  116.5 0.1 copy-done.1
  116.6 0.6 copy.26
  (6 shorter events, 0.0 us)
Async XLA Ops:
  1.9 0.7 copy-start.8
  2.6 0.7 copy-start.6
  2.6 0.7 copy-start.7
  3.3 0.7 copy-start.5
  3.3 1.3 %copy-start.2 = (f32[1408]{0:T(1024)S(1)}, f32[1408]{0:T(1024)}, u32[]{:S(2)}) copy-start(f32[1408]{0:T(1024)} %param.18) | copy-start | bytes 16900
  4.5 0.7 copy-start.3
  5.2 0.7 copy-start.4
  6.7 0.7 copy-start.9
  114.3 1.5 %copy-start = (f32[16,1024]{1,0:T(8,128)S(1)}, f32[16,1024]{1,0:T(8,128)}, u32[]{:S(2)}) copy-start(f32[16,1024]{1,0:T(8,128)} %get-tuple-element.7) | copy-start | bytes 196612
  115.8 0.7 copy-start.1

commit v3 on v2

v3 whole, which is shorter than its diff:
```python
import jax
import jax.numpy as jnp
from jax import lax
from jax.experimental import pallas as pl
from jax.experimental.pallas import tpu as pltpu
from jax.sharding import PartitionSpec as P

D = 1408
E = 1024
NY, NZ, NX, NM = 8, 4, 4, 4
MESH = pl.DeviceIdType.MESH
epsilon = 1e-06
F32 = jnp.float32
BF16 = jnp.bfloat16


def position():
    dp = lax.axis_index("dp")
    mp = lax.axis_index("mp")
    return dp // (NZ * NX), (dp // NX) % NZ, dp % NX, mp


def device(y, z, x, m):
    return ((y * NZ + z) * NX + x, m)


def peer_at(axis, step):
    y, z, x, m = position()
    if axis == "y":
        place = (y + step) % NY
        return device(place, z, x, m), place
    if axis == "z":
        place = (z + step) % NZ
        return device(y, place, x, m), place
    if axis == "x":
        place = (x + step) % NX
        return device(y, z, place, m), place
    place = (m + step) % NM
    return device(y, z, x, place), place


SIZES = {"y": NY, "z": NZ, "x": NX, "m": NM}


def greet():
    barrier = pltpu.get_barrier_semaphore()
    total = 0
    for axis, size in SIZES.items():
        for step in range(1, size):
            target, _ = peer_at(axis, step)
            pl.semaphore_signal(barrier, inc=1, device_id=target, device_id_type=MESH)
            total += 1
    return total


class Links:
    def __init__(self, send_sems, recv_sems):
        self.send_sems, self.recv_sems = send_sems, recv_sems
        self.rows = 0
        self.sent = []

    def row(self):
        self.rows += 1
        return self.rows - 1

    def make(self, source, slot, row, send_index, recv_index, target):
        return pltpu.make_async_remote_copy(
            src_ref=source,
            dst_ref=slot,
            send_sem=self.send_sems.at[row, send_index],
            recv_sem=self.recv_sems.at[row, recv_index],
            device_id=target,
            device_id_type=MESH,
        )

    def send(self, source, slot, row, send_index, recv_index, target):
        copy = self.make(source, slot, row, send_index, recv_index, target)
        copy.start()
        self.sent.append(copy)

    def arrive(self, slot, row, recv_index, target):
        self.make(slot, slot, row, 0, recv_index, target).wait_recv()

    def finish(self):
        for copy in self.sent:
            copy.wait_send()


class Exchange:
    def __init__(self, links, axis, source, slots):
        self.links, self.axis, self.slots = links, axis, slots
        self.row = links.row()
        y, z, x, m = position()
        own = {"y": y, "z": z, "x": x, "m": m}[axis]
        for step in range(1, SIZES[axis]):
            target, place = peer_at(axis, step)
            links.send(source(place), slots.at[own], self.row, step, own, target)

    def wait(self):
        for step in range(1, SIZES[self.axis]):
            target, place = peer_at(self.axis, step)
            self.links.arrive(self.slots.at[place], self.row, place, target)


def one_hot(hit):
    return jnp.where(hit, F32(1.0), F32(0.0)).astype(BF16)


def dot(a, b):
    return jnp.dot(a, b, preferred_element_type=F32)


def dot_t(a, b):
    return lax.dot_general(a, b, (((1,), (1,)), ((), ())), preferred_element_type=F32)


def iota(shape, dim):
    return lax.broadcasted_iota(jnp.int32, shape, dim)


def gelu(v):
    return 0.5 * v * (1.0 + lax.erf(v * F32(0.7071067811865476)))


def step_kernel(
    frames_hbm,
    counts_hbm,
    norm_gain_hbm,
    norm_bias_hbm,
    up_shard_hbm,
    up_bias_hbm,
    down_shard_hbm,
    down_bias_hbm,
    final_gain_hbm,
    final_bias_hbm,
    projection_hbm,
    captions_hbm,
    positives_hbm,
    scale_hbm,
    bias_hbm,
    embed_ref,
    video_ref,
    text_ref,
    counts_ref,
    norm_gain_ref,
    norm_bias_ref,
    up_shard_ref,
    up_bias_ref,
    down_shard_ref,
    down_bias_ref,
    final_gain_ref,
    final_bias_ref,
    projection_ref,
    captions_ref,
    positives_ref,
    scale_ref,
    bias_ref,
    norm_rows,
    up_z,
    down_y,
    projection_rows,
    final_rows,
    hidden,
    partial,
    waiting,
    up_x,
    up_y,
    down_x,
    frames_all,
    normed,
    order,
    bias_rows,
    resid,
    chip_out,
    chip_in,
    pair_out,
    pair_in,
    pool_in,
    pool_all,
    raw_in,
    text_first,
    text_rows,
    text_z,
    video_x,
    where_x,
    text_out_y,
    text_in_y,
    text_out_z,
    text_in_z,
    video_out,
    video_in,
    text_sum_y,
    text_sum_z,
    text_part_y,
    text_part_z,
    text_last_y,
    text_last_z,
    mp_in,
    send_sems,
    recv_sems,
    load_sems,
):
    y, z, x, m = position()
    loads = [
        pltpu.make_async_copy(source, target, load_sems.at[index])
        for index, (source, target) in enumerate(
            (
                (up_shard_hbm, up_shard_ref),
                (down_shard_hbm, down_shard_ref),
                (frames_hbm, frames_all.at[m]),
                (captions_hbm, captions_ref),
                (positives_hbm, positives_ref),
                (counts_hbm, counts_ref),
                (norm_gain_hbm, norm_gain_ref),
                (norm_bias_hbm, norm_bias_ref),
                (up_bias_hbm, up_bias_ref),
                (down_bias_hbm, down_bias_ref),
                (final_gain_hbm, final_gain_ref),
                (final_bias_hbm, final_bias_ref),
                (scale_hbm, scale_ref),
                (bias_hbm, bias_ref),
                (projection_hbm, projection_ref),
            )
        )
    ]
    for load in loads:
        load.start()
    greeted = greet()
    half, core = m // 2, m % 2
    chip_mate = half * 2 + (1 - core)
    pair_mate = (1 - half) * 2 + core
    far_mate = (1 - half) * 2 + (1 - core)
    chip_id = device(y, z, x, chip_mate)
    pair_id = device(y, z, x, pair_mate)
    up_id, up_from = peer_at("y", 1)
    down_id, down_from = peer_at("y", NY - 1)
    right_id, right = peer_at("x", 1)
    left_id, left = peer_at("x", NX - 1)
    across = (x + 2) % NX
    links = Links(send_sems, recv_sems)
    loads[0].wait()
    loads[1].wait()
    up_z[z] = jnp.zeros((16, 768), BF16)
    up_z[z, 0:11, :] = up_shard_ref[...]
    down_y[y] = jnp.zeros((16, 768), BF16)
    down_y[y, 0:11, :] = down_shard_ref[...]
    for load in loads[2:]:
        load.wait()
    caption_values = captions_ref[...].astype(F32)
    text_first[y] = caption_values * lax.rsqrt(
        jnp.sum(caption_values * caption_values, axis=-1, keepdims=True) + epsilon
    )
    for row in range(16):
        where_x[x, row : row + 1, :] = jnp.full((1, 128), positives_ref[row], jnp.int32)
    scale = scale_ref[0]
    bias = bias_ref[0]
    for row, vector in enumerate((norm_gain_ref, norm_bias_ref, down_bias_ref)):
        norm_rows[row : row + 1, :] = vector[...].reshape(1, D)
    pl.semaphore_wait(pltpu.get_barrier_semaphore(), greeted)

    gather_up_z = Exchange(links, "z", lambda place: up_z.at[z], up_z)
    gather_down_y = Exchange(links, "y", lambda place: down_y.at[y], down_y)
    frames_row = links.row()
    links.send(frames_all.at[m], frames_all.at[m], frames_row, 0, 0, chip_id)
    gather_text_first = Exchange(links, "y", lambda place: text_first.at[y], text_first)

    def feature_at(position_of):
        from_x = sum((position_of >= 384 * k).astype(jnp.int32) for k in range(1, NX))
        inside = position_of - 384 * from_x
        from_z = sum((inside >= 96 * k).astype(jnp.int32) for k in range(1, NZ))
        inside = inside - 96 * from_z
        from_y = sum((inside >= 11 * k).astype(jnp.int32) for k in range(1, NY))
        feature = ((from_y * NZ + from_z) * NX + from_x) * 11 + inside - 11 * from_y
        return jnp.where(inside < 88, feature, -1)

    feature = feature_at(iota((1, 1536), 1))
    for quarter in range(NM):
        order[quarter] = one_hot(iota((352, 1536), 0) + 352 * quarter == feature)

    def pack(rows, slots):
        slot_of = iota((rows, slots), 1)
        target_row = lax.shift_right_logical(slot_of, 4) * 11 + lax.bitwise_and(slot_of, 15)
        return one_hot((iota((rows, slots), 0) == target_row) & (lax.bitwise_and(slot_of, 15) < 11))

    gather_up_z.wait()
    up_x[x] = dot(pack(48, 64), up_z[...].reshape(64, 768)).astype(BF16)
    gather_up_x = Exchange(links, "x", lambda place: up_x.at[x], up_x)
    pair_rows = (links.row(), links.row())

    def frame_chunk(place, chunk):
        return frames_all.at[place, 128 * chunk : 128 * chunk + 128, :]

    def send_frames(chunk):
        links.send(frame_chunk(m, chunk), frame_chunk(m, chunk), pair_rows[0], chunk, chunk, pair_id)

    def take_frames(chunk):
        block = frame_chunk(pair_mate, chunk)
        links.arrive(block, pair_rows[0], chunk, pair_id)
        links.send(block, block, pair_rows[1], chunk, chunk, chip_id)

    send_frames(0)

    gather_down_y.wait()
    down_x[x, z] = dot(pack(96, 128), down_y[...].reshape(128, 768)).astype(BF16)
    above_id, above = peer_at("z", 1)
    below_id, below = peer_at("z", NZ - 1)
    from_below, from_above, from_far = links.row(), links.row(), links.row()
    from_left, from_right, from_across = links.row(), links.row(), links.row()

    def piece(column, k):
        place = (z + (0, 1, 3, 2)[k // 2]) % NZ
        return down_x.at[column, place, 48 * (k % 2) : 48 * (k % 2) + 48, :]

    def pass_down(k):
        for part in (2 * k, 2 * k + 1):
            links.send(piece(x, part), piece(x, part), from_left, part, part, right_id)
            links.send(piece(x, part), piece(x, part), from_right, part, part, left_id)

    def take_down(k):
        first, second = piece(x, 2 * k), piece(x, 2 * k + 1)
        row = (None, from_above, from_below, from_far)[k]
        links.arrive(first, row, 0, above_id)
        links.arrive(second, row, 1, above_id)
        if k == 1:
            links.send(second, second, from_far, 1, 1, below_id)
        if k == 2:
            links.send(first, first, from_far, 0, 0, above_id)
        pass_down(k)

    def take_side(k):
        links.arrive(piece(left, k), from_left, k, left_id)
        if k % 2 == 0:
            links.send(piece(left, k), piece(left, k), from_across, k, k, right_id)
        links.arrive(piece(right, k), from_right, k, right_id)
        if k % 2 == 1:
            links.send(piece(right, k), piece(right, k), from_across, k, k, left_id)

    for part in range(2):
        links.send(piece(x, part), piece(x, part), from_below, part, part, above_id)
        links.send(piece(x, part), piece(x, part), from_above, part, part, below_id)
    pass_down(0)
    gather_where = Exchange(links, "x", lambda place: where_x.at[x], where_x)

    slot_of = iota((176, 192), 1)
    from_x = (slot_of >= 48).astype(jnp.int32) + (slot_of >= 96).astype(jnp.int32) + (
        slot_of >= 144
    ).astype(jnp.int32)
    inside = slot_of - 48 * from_x
    from_z = (inside >= 11).astype(jnp.int32) + (inside >= 22).astype(jnp.int32) + (
        inside >= 33
    ).astype(jnp.int32)
    target_row = (from_z * 4 + from_x) * 11 + inside - 11 * from_z
    pack_x = one_hot((iota((176, 192), 0) == target_row) & (inside < 44))
    gather_up_x.wait()
    up_y[y] = dot(pack_x, up_x[...].reshape(192, 768)).astype(BF16)
    up_right, up_left = (links.row(), links.row()), (links.row(), links.row())

    def pass_up(step, part):
        rows = slice(0, 96) if part == 0 else slice(96, 176)
        if step < 4 or part == 0:
            ahead = up_y.at[(y - (step - 1) + NY) % NY, rows, :]
            links.send(ahead, ahead, up_right[part], step, step, up_id)
        if step < 4 or part == 1:
            behind = up_y.at[(y + (step - 1)) % NY, rows, :]
            links.send(behind, behind, up_left[part], step, step, down_id)

    def take_up(step, part):
        rows = slice(0, 96) if part == 0 else slice(96, 176)
        if step < 4 or part == 0:
            links.arrive(up_y.at[(y - step + NY) % NY, rows, :], up_right[part], step, up_id)
        if step < 4 or part == 1:
            links.arrive(up_y.at[(y + step) % NY, rows, :], up_left[part], step, down_id)
        if step < 4:
            pass_up(step + 1, part)

    pass_up(1, 0)
    pass_up(1, 1)
    gather_text_first.wait()
    for slot in range(NY):
        text_rows[4 * slot : 4 * slot + 4, :] = text_first[slot]
    text_z[z] = text_rows[...].astype(BF16)
    take_side(0)
    take_side(1)
    take_down(1)
    take_down(2)
    send_frames(1)
    send_frames(2)
    send_frames(3)
    take_up(1, 0)
    take_side(2)
    take_down(3)
    take_up(1, 1)
    take_side(3)
    take_frames(0)
    take_up(2, 0)
    take_side(4)
    take_frames(1)
    links.arrive(frames_all.at[chip_mate], frames_row, 0, chip_id)

    def normalise(step, carry):
        rows = pl.ds(pl.multiple_of(step * 32, 32), 32)
        values = [frames_all[quarter, rows, :].astype(F32) for quarter in range(NM)]
        total = sum(jnp.sum(v, axis=-1, keepdims=True) for v in values)
        squares = sum(jnp.sum(v * v, axis=-1, keepdims=True) for v in values)
        mean = total * F32(1.0 / D)
        factor = lax.rsqrt(squares * F32(1.0 / D) - mean * mean + epsilon)
        for quarter in range(NM):
            normed[quarter, rows, :] = (
                (values[quarter] - mean) * factor * norm_rows[0:1, 352 * quarter : 352 * quarter + 352]
                + norm_rows[1:2, 352 * quarter : 352 * quarter + 352]
            ).astype(BF16)
        return carry

    def normalise_chunk(chunk):
        links.arrive(frame_chunk(far_mate, chunk), pair_rows[1], chunk, chip_id)
        lax.fori_loop(4 * chunk, 4 * chunk + 4, normalise, 0)

    normalise_chunk(0)
    take_side(5)
    take_up(2, 1)
    take_frames(2)
    normalise_chunk(1)
    take_side(6)
    take_up(3, 0)
    take_frames(3)
    gather_text_z = Exchange(links, "z", lambda place: text_z.at[z], text_z)
    normalise_chunk(2)
    take_side(7)
    take_up(3, 1)
    normalise_chunk(3)

    def rows_of(place):
        return pl.ds(pl.multiple_of(place * 128, 128), 128)

    own = jnp.zeros((128, 1536), F32)
    own_bias = jnp.zeros((16, 1536), F32)
    for quarter in range(NM):
        own += dot(frames_all[quarter, rows_of(m), :], order[quarter])
        bias_part = norm_rows[2:3, 352 * quarter : 352 * quarter + 352]
        bias_rows[...] = jnp.zeros((16, 352), F32)
        for digit in range(3):
            rounded = bias_part.astype(BF16).astype(F32)
            bias_rows[digit : digit + 1, :] = rounded
            bias_part = bias_part - rounded
        own_bias += dot(bias_rows[...].astype(BF16), order[quarter])
    own = own + jnp.sum(own_bias, axis=0, keepdims=True)
    for block in range(NX):
        resid[block] = own[:, 384 * block : 384 * block + 384]
    turn = one_hot(iota((1536, 352), 1) + 352 * m == feature_at(iota((1536, 1), 0)))
    projection_rows[...] = dot(turn, projection_ref[...]).astype(BF16)
    bias_rows[...] = jnp.zeros((16, 352), F32)
    for row, vector in enumerate((final_gain_ref, final_bias_ref)):
        rest = vector[...].reshape(1, 352)
        for part in range(3):
            rounded = rest.astype(BF16).astype(F32)
            bias_rows[3 * row + part : 3 * row + part + 1, :] = rounded
            rest = rest - rounded
    final_parts = dot(bias_rows[...].astype(BF16), order[m])
    final_rows[0:1, :] = jnp.sum(final_parts[0:3, :], axis=0, keepdims=True)
    final_rows[1:2, :] = jnp.sum(final_parts[3:6, :], axis=0, keepdims=True)
    take_up(4, 0)
    take_up(4, 1)
    arrival = [x, left, right, across]

    def hidden_of(side):
        rows = pl.ds(pl.multiple_of(side * 256, 256), 256)
        total = jnp.broadcast_to(up_bias_ref[...].reshape(1, 768), (256, 768))
        for quarter in range(NM):
            total += dot(
                normed[quarter, rows, :],
                up_y[2 * quarter : 2 * quarter + 2].reshape(352, 768),
            )
        hidden[...] = gelu(total).astype(BF16)

    def partial_sums(block):
        sums = dot_t(hidden[...], down_x[block].reshape(384, 768))
        partial[0] = sums[0:128]
        partial[1] = sums[128:256]

    chip_rows, pair_row = (links.row(), links.row()), links.row()

    def pass_pair(k):
        links.arrive(chip_in.at[0, k], chip_rows[0], k, chip_id)
        pair_out[k] = (waiting[k] + chip_in[0, k].astype(F32)).astype(BF16)
        links.send(pair_out.at[k], pair_in.at[k], pair_row, k, k, pair_id)

    hidden_of(1 - half)
    for k, block in enumerate(arrival):
        if k == 3:
            for part in range(2 * NZ):
                links.arrive(piece(across, part), from_across, part, right_id)
        partial_sums(block)
        chip_out[0, k] = partial[1 - core].astype(BF16)
        links.send(chip_out.at[0, k], chip_in.at[0, k], chip_rows[0], k, k, chip_id)
        waiting[k] = partial[core]
        if k > 0:
            pass_pair(k - 1)
    pass_pair(3)
    hidden_of(half)
    for k, block in enumerate(arrival):
        partial_sums(block)
        chip_out[1, k] = partial[1 - core].astype(BF16)
        links.send(chip_out.at[1, k], chip_in.at[1, k], chip_rows[1], k, k, chip_id)
        resid[block] += partial[core]
    for k, block in enumerate(arrival):
        links.arrive(chip_in.at[1, k], chip_rows[1], k, chip_id)
        resid[block] += chip_in[1, k].astype(F32)
    gather_text_z.wait()
    gather_where.wait()
    for k, block in enumerate(arrival):
        links.arrive(pair_in.at[k], pair_row, k, pair_id)
        resid[block] += pair_in[k].astype(F32)

    for clip in range(4):
        rows = slice(32 * clip, 32 * clip + 32)
        values = [resid[block, rows, :] for block in range(NX)]
        total = sum(jnp.sum(v, axis=-1, keepdims=True) for v in values)
        squares = sum(jnp.sum(v * v, axis=-1, keepdims=True) for v in values)
        mean = total * F32(1.0 / D)
        factor = lax.rsqrt(squares * F32(1.0 / D) - mean * mean + epsilon)
        count = jnp.full((32, 1), counts_ref[m * 4 + clip], jnp.int32)
        weight = jnp.where(iota((32, 1), 0) < count, factor / count.astype(F32), F32(0.0))
        for block in range(NX):
            lanes = slice(384 * block, 384 * block + 384)
            pool_in[m, clip : clip + 1, lanes] = jnp.sum(
                (values[block] - mean) * weight, axis=0, keepdims=True
            )
    share_pool = Exchange(links, "m", lambda place: pool_in.at[m], pool_in)
    share_pool.wait()
    for slot in range(NM):
        pool_all[4 * slot : 4 * slot + 4, :] = pool_in[slot]
    pooled = (pool_all[...] * final_rows[0:1, :] + final_rows[1:2, :]).astype(BF16)
    raw_in[m] = dot(pooled, projection_rows[...]).astype(BF16)
    share_raw = Exchange(links, "m", lambda place: raw_in.at[m], raw_in)
    share_raw.wait()
    raw = raw_in[0].astype(F32)
    for slot in range(1, NM):
        raw += raw_in[slot].astype(F32)

    embed = raw * lax.rsqrt(jnp.sum(raw * raw, axis=-1, keepdims=True) + epsilon)
    embed_ref[...] = embed
    video_x[x] = embed.astype(BF16)
    gather_video = Exchange(links, "x", lambda place: video_x.at[x], video_x)
    column = iota((NX * 16, NY * 16), 1)
    owner = lax.bitwise_and(lax.shift_right_logical(column, 2), 7) * NZ + lax.shift_right_logical(column, 5)
    ids = (((owner * 4) + x) * 4 + m) * 4 + lax.bitwise_and(column, 3)
    labels = jnp.where(ids == where_x[...].reshape(NX * 16, 128), F32(1.0), F32(-1.0))
    text = text_z[...].reshape(NY * 16, E)
    row_of = iota((128, 128), 0)
    moved = (
        lax.bitwise_and(lax.shift_right_logical(row_of, 2), 3) * 32
        + lax.shift_right_logical(row_of, 4) * 4
        + lax.bitwise_and(row_of, 3)
    )
    reorder = one_hot(iota((128, 128), 1) == moved)
    gather_video.wait()
    video = video_x[...].reshape(NX * 16, E)
    logits = scale * dot_t(video, text) + bias
    pair_weights = -labels * lax.logistic(-labels * logits)
    turned = jnp.transpose(pair_weights).astype(BF16)
    by_y = dot(reorder, turned).astype(BF16)
    text_out_y[...] = (scale * dot(by_y, video[:, 0:512])).astype(BF16).reshape(NY, 16, 512)
    text_in_y[y] = text_out_y[y]
    reduce_first_y = Exchange(links, "y", lambda place: text_out_y.at[place], text_in_y)
    text_out_z[...] = (scale * dot(turned, video[:, 512:1024])).astype(BF16).reshape(NZ, 32, 512)
    text_in_z[z] = text_out_z[z]
    reduce_first_z = Exchange(links, "z", lambda place: text_out_z.at[place], text_in_z)
    video_out[...] = (scale * dot(pair_weights.astype(BF16), text)).astype(BF16).reshape(NX, 16, E)
    video_in[x] = video_out[x]
    reduce_video_x = Exchange(links, "x", lambda place: video_out.at[place], video_in)

    reduce_video_x.wait()
    video_total = video_in[0].astype(F32)
    for slot in range(1, NX):
        video_total += video_in[slot].astype(F32)
    mp_in[m] = video_total.astype(BF16)
    share_video = Exchange(links, "m", lambda place: mp_in.at[m], mp_in)
    reduce_first_z.wait()
    text_total = text_in_z[0].astype(F32)
    for slot in range(1, NZ):
        text_total += text_in_z[slot].astype(F32)
    text_sum_z[...] = text_total
    for slot in range(NY):
        text_part_y[slot] = text_sum_z[4 * slot : 4 * slot + 4, :]
    text_last_y[y] = text_part_y[y]
    reduce_last_y = Exchange(links, "y", lambda place: text_part_y.at[place], text_last_y)
    reduce_first_y.wait()
    text_total = text_in_y[0].astype(F32)
    for slot in range(1, NY):
        text_total += text_in_y[slot].astype(F32)
    text_sum_y[...] = text_total
    for slot in range(NZ):
        text_part_z[slot] = text_sum_y[4 * slot : 4 * slot + 4, :]
    text_last_z[z] = text_part_z[z]
    reduce_last_z = Exchange(links, "z", lambda place: text_part_z.at[place], text_last_z)
    share_video.wait()
    video_grad = mp_in[0].astype(F32)
    for slot in range(1, NM):
        video_grad += mp_in[slot].astype(F32)
    video_ref[...] = video_grad
    reduce_last_y.wait()
    text_grad = text_last_y[0]
    for slot in range(1, NY):
        text_grad += text_last_y[slot]
    text_ref[:, 512:1024] = text_grad
    reduce_last_z.wait()
    text_grad = text_last_z[0]
    for slot in range(1, NZ):
        text_grad += text_last_z[slot]
    text_ref[:, 0:512] = text_grad
    links.finish()


def on_device(
    frames,
    frame_counts,
    norm_gain,
    norm_bias,
    up_weight,
    up_bias,
    down_weight,
    down_bias,
    final_gain,
    final_bias,
    projection,
    captions,
    positives,
    logit_scale,
    logit_bias,
):
    vmem = pl.BlockSpec(memory_space=pltpu.VMEM)
    hbm = pl.BlockSpec(memory_space=pltpu.HBM)
    return pl.pallas_call(
        step_kernel,
        out_shape=(
            jax.ShapeDtypeStruct((16, E), F32),
            jax.ShapeDtypeStruct((16, E), F32),
            jax.ShapeDtypeStruct((4, E), F32),
        ),
        in_specs=[hbm] * 15,
        out_specs=(vmem, vmem, vmem),
        scratch_shapes=[
            pltpu.SMEM((16,), jnp.int32),
            pltpu.VMEM((D,), F32),
            pltpu.VMEM((D,), F32),
            pltpu.VMEM((11, 768), BF16),
            pltpu.VMEM((768,), F32),
            pltpu.VMEM((11, 768), BF16),
            pltpu.VMEM((D,), F32),
            pltpu.VMEM((352,), F32),
            pltpu.VMEM((352,), F32),
            pltpu.VMEM((352, E), BF16),
            pltpu.VMEM((4, E), BF16),
            pltpu.SMEM((16,), jnp.int32),
            pltpu.SMEM((1,), F32),
            pltpu.SMEM((1,), F32),
            pltpu.VMEM((8, D), F32),
            pltpu.VMEM((NZ, 16, 768), BF16),
            pltpu.VMEM((NY, 16, 768), BF16),
            pltpu.VMEM((1536, E), BF16),
            pltpu.VMEM((8, 1536), F32),
            pltpu.VMEM((256, 768), BF16),
            pltpu.VMEM((2, 128, 384), F32),
            pltpu.VMEM((NX, 128, 384), F32),
            pltpu.VMEM((NX, 48, 768), BF16),
            pltpu.VMEM((NY, 176, 768), BF16),
            pltpu.VMEM((NX, NZ, 96, 768), BF16),
            pltpu.VMEM((NM, 512, 352), BF16),
            pltpu.VMEM((NM, 512, 352), BF16),
            pltpu.VMEM((NM, 352, 1536), BF16),
            pltpu.VMEM((16, 352), F32),
            pltpu.VMEM((NX, 128, 384), F32),
            pltpu.VMEM((2, NX, 128, 384), BF16),
            pltpu.VMEM((2, NX, 128, 384), BF16),
            pltpu.VMEM((NX, 128, 384), BF16),
            pltpu.VMEM((NX, 128, 384), BF16),
            pltpu.VMEM((NM, 4, 1536), F32),
            pltpu.VMEM((16, 1536), F32),
            pltpu.VMEM((NM, 16, E), BF16),
            pltpu.VMEM((NY, 4, E), F32),
            pltpu.VMEM((32, E), F32),
            pltpu.VMEM((NZ, 32, E), BF16),
            pltpu.VMEM((NX, 16, E), BF16),
            pltpu.VMEM((NX, 16, 128), jnp.int32),
            pltpu.VMEM((NY, 16, 512), BF16),
            pltpu.VMEM((NY, 16, 512), BF16),
            pltpu.VMEM((NZ, 32, 512), BF16),
            pltpu.VMEM((NZ, 32, 512), BF16),
            pltpu.VMEM((NX, 16, E), BF16),
            pltpu.VMEM((NX, 16, E), BF16),
            pltpu.VMEM((16, 512), F32),
            pltpu.VMEM((32, 512), F32),
            pltpu.VMEM((NY, 4, 512), F32),
            pltpu.VMEM((NZ, 4, 512), F32),
            pltpu.VMEM((NY, 4, 512), F32),
            pltpu.VMEM((NZ, 4, 512), F32),
            pltpu.VMEM((NM, 16, E), BF16),
            pltpu.SemaphoreType.DMA((36, 8)),
            pltpu.SemaphoreType.DMA((36, 8)),
            pltpu.SemaphoreType.DMA((15,)),
        ],
        compiler_params=pltpu.CompilerParams(
            collective_id=0, has_side_effects=True, vmem_limit_bytes=56 * 1024 * 1024
        ),
    )(
        frames.reshape(512, 352),
        frame_counts,
        norm_gain,
        norm_bias,
        up_weight,
        up_bias,
        down_weight,
        down_bias,
        final_gain,
        final_bias,
        projection,
        captions,
        positives,
        logit_scale.reshape(1),
        logit_bias.reshape(1),
    )


def solution(mesh):
    return jax.shard_map(
        on_device,
        mesh=mesh,
        in_specs=(
            P("dp", None, "mp"),
            P("dp"),
            P(),
            P(),
            P("dp", "mp"),
            P("mp"),
            P("dp", "mp"),
            P(),
            P("mp"),
            P("mp"),
            P("mp", None),
            P(("dp", "mp"), None),
            P("dp"),
            P(),
            P(),
        ),
        out_specs=(P("dp", None), P("dp", None), P(("dp", "mp"), None)),
        check_vma=False,
    )
```

time: 119 us -> 96.5 us (0.81); the launches traced: 117 us -> 96.3 us
  Pallas kernels: 105 us -> 91.5 us
  local copies, waits for them, and re-layouts: 7.81 us -> 2.83 us
  other arithmetic: 1.96 us -> 0 us
    pallas_call x1, Pallas kernels: 105 us -> 91.5 us  [on_device(): pl.pallas_call(step_kernel, out_shape=(jax.ShapeDtypeStruct((16, E), F32)...]
    unnamed x23 -> x7, local copies, waits for them, and re-layouts: 5.38 us -> 2.83 us
    another operation x3 -> x0, other arithmetic: 1.88 us -> none  [the longest x1 0.65 us: on_device(): jnp.stack([logit_scale, logit_bias])]
    broadcast_in_dim x2 -> x0, local copies, waits for them, and re-layouts: 1.51 us -> none  [the longest x1 0.84 us: on_device(): weights = jnp.broadcast_to(weights.reshape(512, 1), (512, 128))]
where the time goes in v3:
time: 96.5 us; the launch traced here: 96.3 us
  Pallas kernels  91.5 us (95%)
  local copies, waits for them, and re-layouts  2.83 us (3%)
  between operations  1.95 us (2%)
    pallas_call x1, Pallas kernels, on_device(): pl.pallas_call(step_kernel, out_shape=(jax.ShapeDtypeStruct((16, E), F32)...  91.5 us
    unnamed x7, local copies, waits for them, and re-layouts  2.83 us

profile of v3, /device:TPU:6, one launch (start us, length us, event | category | flops | bytes accessed | tf_op | source)
XLA Modules:
  0.0 96.3 jit_solution(5288745688610669139)
XLA Ops:
  1.9 91.5 %shard_map.166 = (f32[16,1024]{1,0:T(8,128)}, f32[16,1024]{1,0:T(8,128)}, f32[4,1024]{1,0:T(4,128)}) custom-call(bf16[512,352]{1,0:T(8,128)(2,1)} %bitcast.5, s32[16]{0:T(128)} %counts_hbm.1, f32[1408]{0:T(1024)} %norm_gain_hbm.1, f32[1408]{0:T(1024)} %norm_bias_hbm.1, bf16[11,768]{1,0:T(8,128)(2,1)} %up_shard_hbm.1, f32[768]{0:T(1024)} %up_bias_hbm.1, ...), custom_call_target="tpu_custom_call" | custom-call | tf_op jit(solution)/shard_map/pallas_call | solution.py:633
  93.4 0.0 copy-start
  93.4 1.5 %copy.23 = f32[16,1024]{1,0:T(8,128)} copy(f32[16,1024]{1,0:T(8,128)} %get-tuple-element.6) | data formatting | bytes 131072
  95.0 0.0 copy-done
  95.0 0.0 copy-start.1
  95.0 0.6 copy.24
  95.6 0.1 copy-done.1
  95.7 0.6 copy.25
Async XLA Ops:
  93.4 1.5 %copy-start = (f32[16,1024]{1,0:T(8,128)S(1)}, f32[16,1024]{1,0:T(8,128)}, u32[]{:S(2)}) copy-start(f32[16,1024]{1,0:T(8,128)} %get-tuple-element.7) | copy-start | bytes 196612
  95.0 0.7 copy-start.1

commit v4 on v3

--- a/solution.py
+++ b/solution.py
@@ -223,9 +223,11 @@
             )
         )
     ]
-    for load in loads:
+    loads[0].start()
+    loads[1].start()
+    greeted = greet()
+    for load in loads[2:]:
         load.start()
-    greeted = greet()
     half, core = m // 2, m % 2
     chip_mate = half * 2 + (1 - core)
     pair_mate = (1 - half) * 2 + core
@@ -244,6 +246,10 @@
     up_z[z, 0:11, :] = up_shard_ref[...]
     down_y[y] = jnp.zeros((16, 768), BF16)
     down_y[y, 0:11, :] = down_shard_ref[...]
+    pl.semaphore_wait(pltpu.get_barrier_semaphore(), greeted)
+
+    gather_up_z = Exchange(links, "z", lambda place: up_z.at[z], up_z)
+    gather_down_y = Exchange(links, "y", lambda place: down_y.at[y], down_y)
     for load in loads[2:]:
         load.wait()
     caption_values = captions_ref[...].astype(F32)
@@ -256,13 +262,8 @@
     bias = bias_ref[0]
     for row, vector in enumerate((norm_gain_ref, norm_bias_ref, down_bias_ref)):
         norm_rows[row : row + 1, :] = vector[...].reshape(1, D)
-    pl.semaphore_wait(pltpu.get_barrier_semaphore(), greeted)
-
-    gather_up_z = Exchange(links, "z", lambda place: up_z.at[z], up_z)
-    gather_down_y = Exchange(links, "y", lambda place: down_y.at[y], down_y)
     frames_row = links.row()
     links.send(frames_all.at[m], frames_all.at[m], frames_row, 0, 0, chip_id)
-    gather_text_first = Exchange(links, "y", lambda place: text_first.at[y], text_first)
 
     def feature_at(position_of):
         from_x = sum((position_of >= 384 * k).astype(jnp.int32) for k in range(1, NX))
@@ -273,10 +274,6 @@
         feature = ((from_y * NZ + from_z) * NX + from_x) * 11 + inside - 11 * from_y
         return jnp.where(inside < 88, feature, -1)
 
-    feature = feature_at(iota((1, 1536), 1))
-    for quarter in range(NM):
-        order[quarter] = one_hot(iota((352, 1536), 0) + 352 * quarter == feature)
-
     def pack(rows, slots):
         slot_of = iota((rows, slots), 1)
         target_row = lax.shift_right_logical(slot_of, 4) * 11 + lax.bitwise_and(slot_of, 15)
@@ -301,6 +298,7 @@
     send_frames(0)
 
     gather_down_y.wait()
+    gather_text_first = Exchange(links, "y", lambda place: text_first.at[y], text_first)
     down_x[x, z] = dot(pack(96, 128), down_y[...].reshape(128, 768)).astype(BF16)
     above_id, above = peer_at("z", 1)
     below_id, below = peer_at("z", NZ - 1)
@@ -339,6 +337,9 @@
         links.send(piece(x, part), piece(x, part), from_below, part, part, above_id)
         links.send(piece(x, part), piece(x, part), from_above, part, part, below_id)
     pass_down(0)
+    feature = feature_at(iota((1, 1536), 1))
+    for quarter in range(NM):
+        order[quarter] = one_hot(iota((352, 1536), 0) + 352 * quarter == feature)
     gather_where = Exchange(links, "x", lambda place: where_x.at[x], where_x)
 
     slot_of = iota((176, 192), 1)
@@ -379,24 +380,6 @@
     for slot in range(NY):
         text_rows[4 * slot : 4 * slot + 4, :] = text_first[slot]
     text_z[z] = text_rows[...].astype(BF16)
-    take_side(0)
-    take_side(1)
-    take_down(1)
-    take_down(2)
-    send_frames(1)
-    send_frames(2)
-    send_frames(3)
-    take_up(1, 0)
-    take_side(2)
-    take_down(3)
-    take_up(1, 1)
-    take_side(3)
-    take_frames(0)
-    take_up(2, 0)
-    take_side(4)
-    take_frames(1)
-    links.arrive(frames_all.at[chip_mate], frames_row, 0, chip_id)
-
     def normalise(step, carry):
         rows = pl.ds(pl.multiple_of(step * 32, 32), 32)
         values = [frames_all[quarter, rows, :].astype(F32) for quarter in range(NM)]
@@ -415,18 +398,35 @@
         links.arrive(frame_chunk(far_mate, chunk), pair_rows[1], chunk, chip_id)
         lax.fori_loop(4 * chunk, 4 * chunk + 4, normalise, 0)
 
+    take_side(0)
+    take_side(1)
+    take_up(1, 0)
+    take_down(1)
+    take_down(2)
+    send_frames(1)
+    send_frames(2)
+    send_frames(3)
+    take_up(1, 1)
+    take_side(2)
+    take_side(3)
+    take_frames(0)
+    links.arrive(frames_all.at[chip_mate], frames_row, 0, chip_id)
+    take_up(2, 0)
+    take_side(4)
+    take_frames(1)
     normalise_chunk(0)
+    take_up(2, 1)
     take_side(5)
-    take_up(2, 1)
+    take_down(3)
     take_frames(2)
-    normalise_chunk(1)
-    take_side(6)
-    take_up(3, 0)
     take_frames(3)
     gather_text_z = Exchange(links, "z", lambda place: text_z.at[z], text_z)
+    normalise_chunk(1)
+    take_up(3, 0)
+    take_side(6)
     normalise_chunk(2)
+    take_up(3, 1)
     take_side(7)
-    take_up(3, 1)
     normalise_chunk(3)
 
     def rows_of(place):
@@ -507,17 +507,20 @@
         resid[block] += chip_in[1, k].astype(F32)
     gather_text_z.wait()
     gather_where.wait()
+    total, squares = jnp.zeros((128, 1), F32), jnp.zeros((128, 1), F32)
     for k, block in enumerate(arrival):
         links.arrive(pair_in.at[k], pair_row, k, pair_id)
-        resid[block] += pair_in[k].astype(F32)
+        values = resid[block] + pair_in[k].astype(F32)
+        resid[block] = values
+        total += jnp.sum(values, axis=-1, keepdims=True)
+        squares += jnp.sum(values * values, axis=-1, keepdims=True)
+    means = total * F32(1.0 / D)
+    factors = lax.rsqrt(squares * F32(1.0 / D) - means * means + epsilon)
 
     for clip in range(4):
         rows = slice(32 * clip, 32 * clip + 32)
         values = [resid[block, rows, :] for block in range(NX)]
-        total = sum(jnp.sum(v, axis=-1, keepdims=True) for v in values)
-        squares = sum(jnp.sum(v * v, axis=-1, keepdims=True) for v in values)
-        mean = total * F32(1.0 / D)
-        factor = lax.rsqrt(squares * F32(1.0 / D) - mean * mean + epsilon)
+        mean, factor = means[rows], factors[rows]
         count = jnp.full((32, 1), counts_ref[m * 4 + clip], jnp.int32)
         weight = jnp.where(iota((32, 1), 0) < count, factor / count.astype(F32), F32(0.0))
         for block in range(NX):

time: 96.5 us -> 97.3 us (level)
  the two profiles are of different devices: /device:TPU:6 before, /device:TPU:16 now
where the time goes in v4:
time: 97.3 us; the launch traced here: 97.1 us
  Pallas kernels  92.3 us (95%)
  local copies, waits for them, and re-layouts  2.83 us (3%)
  between operations  1.95 us (2%)
    pallas_call x1, Pallas kernels, on_device(): pl.pallas_call(step_kernel, out_shape=(jax.ShapeDtypeStruct((16, E), F32)...  92.3 us
    unnamed x7, local copies, waits for them, and re-layouts  2.83 us

profile of v4, /device:TPU:16, one launch (start us, length us, event | category | flops | bytes accessed | tf_op | source)
XLA Modules:
  0.0 97.1 jit_solution(7888620309737661981)
XLA Ops:
  1.9 92.3 %shard_map.166 = (f32[16,1024]{1,0:T(8,128)}, f32[16,1024]{1,0:T(8,128)}, f32[4,1024]{1,0:T(4,128)}) custom-call(bf16[512,352]{1,0:T(8,128)(2,1)} %bitcast.5, s32[16]{0:T(128)} %counts_hbm.1, f32[1408]{0:T(1024)} %norm_gain_hbm.1, f32[1408]{0:T(1024)} %norm_bias_hbm.1, bf16[11,768]{1,0:T(8,128)(2,1)} %up_shard_hbm.1, f32[768]{0:T(1024)} %up_bias_hbm.1, ...), custom_call_target="tpu_custom_call" | custom-call | tf_op jit(solution)/shard_map/pallas_call | solution.py:636
  94.2 0.0 copy-start
  94.2 1.5 %copy.23 = f32[16,1024]{1,0:T(8,128)} copy(f32[16,1024]{1,0:T(8,128)} %get-tuple-element.6) | data formatting | bytes 131072
  95.7 0.0 copy-done
  95.7 0.0 copy-start.1
  95.7 0.6 copy.24
  96.4 0.1 copy-done.1
  96.5 0.6 copy.25
Async XLA Ops:
  94.2 1.5 %copy-start = (f32[16,1024]{1,0:T(8,128)S(1)}, f32[16,1024]{1,0:T(8,128)}, u32[]{:S(2)}) copy-start(f32[16,1024]{1,0:T(8,128)} %get-tuple-element.7) | copy-start | bytes 196612
  95.7 0.7 copy-start.1
